TPU v7x, 256 devices: a whole 4x4x8 slice. The times are simulated.
256 devices in a mesh: pool: 2 (over y_hi), band: 8 (over x, core), fft: 16 (over z, y_lo).
Axes of the slice: x: 4, y: 4 (y_hi: 2, y_lo: 2; y = y_hi * 2 + y_lo), z: 8, core: 2. Of those that a mesh axis runs over, the one named last changes fastest.
Arguments:
- coefficients: float32 [2, 32, 2, 221184], P('pool', 'band', None, 'fft'), may hold values from -6 to 6
- occupation: float32 [2, 32], P('pool', 'band'), may hold values from 0.1 to 2
- kpoint_weight: int32 [2], replicated, may hold values from 1 to 8
- stick_cell: int32 [2304], P('fft'), may hold values from 0 to 9215, as said below
- species: int32 [128], replicated, may hold values from 0 to 2
- positions: float32 [3, 128], replicated, may hold values from 0 to 1
- amplitude: float32 [3], replicated, may hold values from 30 to 300
- core_width: float32 [3], replicated, may hold values from 0.3 to 1
Outputs:
- forces: float32 [3, 128], replicated
Inputs may be any that keep to these rules, and one draw needn't show every extreme that they name: `stick_cell`: the entries are distinct cells. Every cell with 16 m_x^2 + 16 m_y^2 <= 96^2 is among them, the others lie outside that disk; each block of 144 entries (one index of fft) holds the disk's cells to within one of an equal share.
All inputs are finite; a program needn't handle non-finite values.
Results may differ from a plain program's by a relative error of at most 0.0003.
Values sent between devices are 32-bit elements; how exact they have to be, the bound alone decides.
No kernel may reach another device: no remote copies, remote signals or barrier semaphores. Data moves between devices by JAX's collectives and lax.ppermute only.
A program may use at most 128 MiB of HBM per device.

v0:
```python
import math

import jax
import jax.numpy as jnp
import numpy as np
from jax import lax
from jax.experimental import pallas as pl
from jax.experimental.pallas import tpu as pltpu
from jax.sharding import PartitionSpec as P

NX = 96
NY = 96
NZ = 192
ZSPAN = 96
NGRID = 1769472
HALF = 24
SIDE = 49
LANES = 128
PLANES = 12
SLOTS = 25
SIDE_ROWS = SLOTS * 16
HIGH = lax.Precision.HIGH
screen = 0.25
VMEM = pl.BlockSpec(memory_space=pltpu.VMEM)
SMEM = pl.BlockSpec(memory_space=pltpu.SMEM)


def signed_freq(offsets, length):
    return (offsets + length // 2) % length - length // 2


def trig(rows, columns, length):
    angles = 2.0 * np.pi / length * (np.outer(rows, columns) % length)
    return np.cos(angles).astype(np.float32), np.sin(angles).astype(np.float32)


def halves(values):
    high = values.astype(jnp.bfloat16)
    return high, (values - high.astype(jnp.float32)).astype(jnp.bfloat16)


def table_halves(values):
    high = lax.reduce_precision(values, 8, 7)
    return high.astype(jnp.bfloat16), (values - high).astype(jnp.bfloat16)


def np_halves(values):
    high = values.astype(jnp.bfloat16)
    return high, (values - high.astype(np.float32)).astype(jnp.bfloat16)


def mm(left, right):
    return jnp.dot(left, right, preferred_element_type=jnp.float32)


def z_table():
    cosine, sine = trig(np.arange(NZ), np.arange(ZSPAN) - NZ // 4, NZ)
    real_rows = np.stack([cosine, -sine], 1)
    imag_rows = np.stack([sine, cosine], 1)
    table = np.stack([real_rows, imag_rows], 1)
    return table.reshape(16, PLANES, 2, 2, ZSPAN)


def inverse_y_tables():
    cosine, sine = trig(np.arange(SIDE) - HALF, np.arange(96), 96)
    both = np.zeros((SIDE, 256), np.float32)
    both[:, :96], both[:, 128:224] = cosine, sine
    high, low = np_halves(both)
    first = np.zeros((2, 256, 256), high.dtype)
    second = np.zeros((2, 128, 256), high.dtype)
    for half in range(2):
        for part in range(2):
            first[half, 128 * part + 64 * half : 128 * part + 64 * half + SIDE] = high
        second[half, 64 * half : 64 * half + SIDE] = low
    return first, second


def inverse_x_table():
    cosine, sine = trig(np.arange(96), np.arange(SIDE) - HALF, 96)
    both = np.zeros((192, 64), np.float32)
    both[:96, :SIDE], both[96:, :SIDE] = cosine, sine
    high, low = np_halves(both)
    return np.concatenate([high, high, low], 1)


def forward_y_tables():
    cosine, sine = trig(np.arange(96), np.arange(SIDE), 96)
    both = np.zeros((128, 128), np.float32)
    both[:96, :SIDE], both[:96, 64 : 64 + SIDE] = cosine, sine
    high, low = np_halves(both)
    return np.concatenate([high, high], 0), low


def forward_x_tables():
    cosine, sine = trig(np.arange(50), np.arange(96), 96)
    cosine[SIDE:], sine[SIDE:] = 0.0, 0.0
    result = []
    for core in range(2):
        both = np.zeros((128, 96), np.float32)
        for index, rows in enumerate((core, 1 - core)):
            both[64 * index : 64 * index + SLOTS] = cosine[rows::2]
            both[64 * index + 32 : 64 * index + 32 + SLOTS] = sine[rows::2]
        high, low = np_halves(both)
        result.append(np.concatenate([high, high, low], 1))
    return np.stack(result)


def density_kernel(
    factors, recv, inv_y1, inv_y2, inv_x, fwd_y1, fwd_y2, fwd_x, own, other, parts, ids, held_re, held_im
):
    for source in range(16):
        high, low = halves(recv[source, :96, :])
        parts[:96, source * LANES : (source + 1) * LANES] = high
        parts[96:, source * LANES : (source + 1) * LANES] = low
        ids[:, source * LANES : (source + 1) * LANES] = recv[source, 96:104, :].astype(jnp.int32)
    blank = jnp.zeros((48, 128), jnp.float32)
    for row in range(52, 64):
        held_re[pl.ds(row, 48, stride=64), :] = blank
        held_im[pl.ds(row, 48, stride=64), :] = blank

    def place(tile, _):
        cells = lax.broadcasted_iota(jnp.int32, (256, 256), 0) + tile * 256
        total = jnp.zeros((192, 256), jnp.float32)
        for block in range(8):
            span = slice(block * 256, block * 256 + 256)
            spots = (cells == ids[0:1, span]).astype(jnp.float32).astype(jnp.bfloat16)
            total = total + lax.dot_general(
                parts[:, span], spots, (((1,), (1,)), ((), ())), preferred_element_type=jnp.float32
            )
        grid = total[:96] + total[96:]
        high, low = halves(grid)
        for column in range(4):
            pair = slice((column // 2) * 128, (column // 2) * 128 + 128)
            both = jnp.concatenate([high[:, pair], low[:, pair]], 1)
            out = mm(both, inv_y1[column % 2]) + mm(high[:, pair], inv_y2[column % 2])
            rows = pl.ds(tile * 4 + column, 48, stride=64)
            held_re[rows, :] = out[:48, :128] - out[48:, 128:]
            held_im[rows, :] = out[48:, :128] + out[:48, 128:]
        return 0

    lax.fori_loop(0, 13, place, 0)
    clear = jnp.zeros((2 * SLOTS, 128), jnp.float32)
    for row in range(PLANES, 16):
        own[pl.ds(row, 2 * SLOTS, stride=16), :] = clear
        other[pl.ds(row, 2 * SLOTS, stride=16), :] = clear

    def plane_step(plane, _):
        density = jnp.zeros((96, 128), jnp.float32)
        for band in range(4):
            start = pl.multiple_of((band * PLANES + plane) * 64, 64)
            rows = pl.ds(start, 64)
            high, low = halves(jnp.concatenate([held_re[rows, :], held_im[rows, :]], 1))
            out = mm(inv_x[...], jnp.concatenate([high, low, high], 0))
            wave_re = out[:96, :128] - out[96:, 128:]
            wave_im = out[96:, :128] + out[:96, 128:]
            density = density + factors[band] * (wave_re * wave_re + wave_im * wave_im)
        high, low = halves(density)
        rows = mm(jnp.concatenate([high, low], 1), fwd_y1[...]) + mm(high, fwd_y2[...])
        high, low = halves(rows)
        out = mm(fwd_x[...], jnp.concatenate([high, low, high], 0))
        first, second = pl.ds(plane, SLOTS, stride=16), pl.ds(plane + SIDE_ROWS, SLOTS, stride=16)
        own[first, :] = out[0:SLOTS]
        own[second, :] = out[32 : 32 + SLOTS]
        other[first, :] = out[64 : 64 + SLOTS]
        other[second, :] = out[96 : 96 + SLOTS]
        return 0

    lax.fori_loop(0, PLANES, plane_step, 0)


def force_kernel(gx2, own, arrived, base, wave_z, atom_z, x_all, y_cos, y_sin, strength, out, acc, turn):
    acc[...] = jnp.zeros_like(acc)
    turn[...] = x_all[...]

    def step(slot, _):
        start = pl.multiple_of(slot * 16, 16)
        first, second = pl.ds(start, 16), pl.ds(start + SIDE_ROWS, 16)
        pair = [own[first, :] + arrived[first, :], own[second, :] + arrived[second, :]]
        high, low = halves(jnp.concatenate(pair, 1))
        raw = mm(wave_z[...], jnp.concatenate([high, low, high], 0))
        weight = 1.0 / (base[...] + gx2[slot])
        weight = jnp.concatenate([weight, weight], 1)
        weight = jnp.concatenate([weight, weight], 0)
        high, low = halves(raw * weight)
        both = mm(atom_z[...], jnp.concatenate([high, low, high], 0))
        table = turn[...]
        xc_c, xc_s = table[:, 0:1], table[:, 32:33]
        xs_c, xs_s = table[:, 64:65], table[:, 96:97]
        plain_c, plain_s = both[:128, :128], both[:128, 128:]
        acc[0] += xs_c * plain_c + xs_s * plain_s
        acc[1] += xc_c * plain_c + xc_s * plain_s
        acc[2] += xc_c * both[128:, :128] + xc_s * both[128:, 128:]
        turn[...] = pltpu.roll(table, 127, 1)
        return 0

    lax.fori_loop(0, SLOTS, step, 0)
    parts = [acc[0] * y_cos[...], acc[1] * y_sin[...], acc[2] * y_cos[...]]
    rows = [-strength[...] * jnp.sum(part.T, axis=0, keepdims=True) for part in parts]
    block = jnp.concatenate(rows + [jnp.zeros((5, 128), jnp.float32)], 0)
    for index in range(16):
        out[index] = block


def shards(
    coefficients, occupation, kpoint_weight, stick_cell, species, positions, amplitude, core_width
):
    sticks = stick_cell.shape[0]
    shaped = coefficients[0].reshape(4, 2, sticks, ZSPAN)
    freq_x = signed_freq(stick_cell // NY, NX)
    freq_y = signed_freq(stick_cell % NY, NY)
    freq_z = jnp.arange(ZSPAN, dtype=jnp.int32) - NZ // 4
    disk = 16 * (freq_x * freq_x + freq_y * freq_y)
    level = disk[:, None] + 4 * (freq_z * freq_z)[None, :]
    masked = jnp.where(level <= NX * NX, shaped, 0.0)
    chosen = disk <= NX * NX
    before = jnp.arange(sticks)[:, None] < jnp.arange(sticks)[None, :]
    rank = jnp.sum(jnp.where(before & chosen[:, None], 1, 0), axis=0)
    lane = jnp.arange(LANES, dtype=jnp.int32)
    pick = (chosen[:, None] & (rank[:, None] == lane[None, :])).astype(jnp.float32)
    place = ((freq_x + HALF) * 64 + freq_y + HALF + 1).astype(jnp.float32)
    ids = jnp.sum(pick * place[:, None], axis=0) - 1.0
    packed = jnp.einsum("bcst,sj->bctj", masked, pick, precision=HIGH)
    planes = jnp.einsum("dpoct,bctj->dobpj", z_table(), packed, precision=HIGH)
    planes = planes.reshape(16, 96, LANES)
    payload = jnp.concatenate([planes, jnp.broadcast_to(ids[None, None], (16, 8, LANES))], 1)
    received = lax.all_to_all(payload, "fft", split_axis=0, concat_axis=0, tiled=True)

    core = lax.axis_index("band") % 2
    pool_weight = lax.dynamic_index_in_dim(
        kpoint_weight, lax.axis_index("pool"), keepdims=False
    ).astype(jnp.float32) / jnp.sum(kpoint_weight).astype(jnp.float32)
    factors = pool_weight * occupation[0] * (16.0 / NGRID / 32.0 / NGRID)
    inv_y1, inv_y2 = inverse_y_tables()
    fwd_y1, fwd_y2 = forward_y_tables()
    fwd_x = lax.dynamic_index_in_dim(jnp.asarray(forward_x_tables()), core, keepdims=False)
    halves_shape = jax.ShapeDtypeStruct((2 * SIDE_ROWS, 128), jnp.float32)
    own, other = pl.pallas_call(
        density_kernel,
        out_shape=(halves_shape, halves_shape),
        in_specs=[SMEM] + [VMEM] * 7,
        out_specs=(VMEM, VMEM),
        scratch_shapes=[
            pltpu.VMEM((192, 2048), jnp.bfloat16),
            pltpu.VMEM((8, 2048), jnp.int32),
            pltpu.VMEM((48 * 64, 128), jnp.float32),
            pltpu.VMEM((48 * 64, 128), jnp.float32),
        ],
        compiler_params=pltpu.CompilerParams(vmem_limit_bytes=40 * 1024 * 1024),
        name="density",
    )(factors, received, inv_y1, inv_y2, inverse_x_table(), fwd_y1, fwd_y2, fwd_x)
    swap = [(index, index ^ 1) for index in range(8)]
    arrived = lax.ppermute(other, "band", swap)

    start = lax.axis_index("fft") * PLANES
    steps = (jnp.arange(ZSPAN)[:, None] * (start + jnp.arange(PLANES))[None, :]) % NZ
    angles = 2.0 * math.pi / NZ * steps.astype(jnp.float32)
    turned = jnp.pad(jnp.concatenate([jnp.cos(angles), jnp.sin(angles)], 0), ((0, 0), (0, 4)))
    high, low = table_halves(turned)
    wave_z = jnp.concatenate([high, high, low], 1)
    kinds = species[None, :] == jnp.arange(3, dtype=jnp.int32)[:, None]
    width = jnp.sum(jnp.where(kinds, core_width[:, None], 0.0), axis=0)
    strength = jnp.sum(jnp.where(kinds, amplitude[:, None], 0.0), axis=0)

    def tables(where, order, unit, counts):
        waves = unit * order
        turns = where[:, None] * order[None, :]
        phase = 2.0 * math.pi * (turns - jnp.round(turns))
        scale = counts[None, :] * jnp.exp(-0.5 * (width * width)[:, None] * (waves * waves)[None])
        cosine, sine = scale * jnp.cos(phase), scale * jnp.sin(phase)
        slope = waves[None, :]
        return cosine, sine, slope * sine, -slope * cosine

    hx = 2.0 * jnp.arange(32, dtype=jnp.float32) + core.astype(jnp.float32)
    unit = 2.0 * math.pi / 96
    count_x = jnp.where(hx > 48.0, 0.0, jnp.where((hx == 0.0) | (hx == 48.0), 1.0, 2.0))
    x_all = jnp.concatenate(tables(positions[0], hx, unit, count_x), 1)
    hy = jnp.arange(64, dtype=jnp.float32)
    count_y = jnp.where(hy > 48.0, 0.0, jnp.where((hy == 0.0) | (hy == 48.0), 1.0, 2.0))
    y_parts = tables(positions[1], hy, unit, count_y)
    y_cos = jnp.concatenate(y_parts[:2], 1)
    y_sin = jnp.concatenate(y_parts[2:], 1)
    hz = jnp.arange(ZSPAN, dtype=jnp.float32)
    z_parts = tables(positions[2], hz, 2.0 * math.pi / NZ, jnp.where(hz == 0.0, 1.0, 2.0))
    z_rows = jnp.concatenate(
        [jnp.concatenate(z_parts[:2], 1), jnp.concatenate(z_parts[2:], 1)], 0
    )
    high, low = table_halves(z_rows)
    atom_z = jnp.concatenate([high, high, low], 1)
    gy = np.tile(2.0 * np.pi / 96 * np.arange(64), 2)
    gz = 2.0 * np.pi / NZ * np.arange(ZSPAN)
    base = (gy[None, :] ** 2 + gz[:, None] ** 2 + screen).astype(np.float32)
    gx2 = (unit * hx) * (unit * hx)
    spread = pl.pallas_call(
        force_kernel,
        out_shape=jax.ShapeDtypeStruct((16, 8, LANES), jnp.float32),
        in_specs=[SMEM] + [VMEM] * 9,
        out_specs=VMEM,
        scratch_shapes=[
            pltpu.VMEM((3, 128, 128), jnp.float32),
            pltpu.VMEM((128, 128), jnp.float32),
        ],
        compiler_params=pltpu.CompilerParams(vmem_limit_bytes=40 * 1024 * 1024),
        name="force",
    )(gx2, own, arrived, base, wave_z, atom_z, x_all, y_cos, y_sin, strength[None])
    total = jnp.sum(lax.all_to_all(spread, ("pool", "band"), 0, 0, tiled=True), axis=0)
    spread = jnp.broadcast_to(total[None], (16, 8, LANES))
    total = jnp.sum(lax.all_to_all(spread, "fft", 0, 0, tiled=True), axis=0)
    return total[:3]


def solution(mesh):
    placed = (P("pool", "band", None, "fft"), P("pool", "band"), P(), P("fft"), P(), P(), P(), P())
    return jax.shard_map(shards, mesh=mesh, in_specs=placed, out_specs=P(), check_vma=False)
```

profile of v0, /device:TPU:1, one launch (start us, length us, event | category | flops | bytes accessed | tf_op | source)
XLA Modules:
  0.0 100.7 jit_solution(1061674895436775275)
XLA Ops:
  0.0 0.7 copy-done.9
  0.8 0.1 select_reduce_fusion.1
  1.0 1.5 %reshape_squeeze.3 = f32[4,2,144,96]{3,2,1,0:T(8,128)S(1)} reshape(f32[1,4,2,13824]{3,2,1,0:T(2,128)} %param.16) | data formatting | bytes 884736 | tf_op jit(solution)/shard_map/reshape;squeeze | solution.py:208
  2.6 0.7 convolution_bitcast_fusion.1
  3.3 0.2 copy-done.6
  3.6 0.5 convolution_bitcast_fusion
  4.2 0.3 copy.27
  4.4 1.0 pad_maximum_fusion
  5.4 10.1 %all-to-all-start = ((f32[16,104,128]{2,1,0:T(8,128)}), f32[16,104,128]{2,1,0:T(8,128)S(1)}, u32[]{:S(2)}, u32[]{:S(2)}) async-start(f32[16,104,128]{2,1,0:T(8,128)} %pad_maximum_fusion), calls=%async_computation | async-start | bytes 1703936 | tf_op jit(solution)/shard_map/all_to_all | solution.py:226
  15.7 0.1 fusion.19
  15.9 0.5 copy-done.10
  16.6 0.7 copy-done.13
  17.2 0.7 reduce_sum.63
  17.9 0.6 dynamic_slice.8
  19.7 0.1 copy.28
  19.9 0.7 copy-done.8
  20.6 0.3 cosine_multiply_fusion.1
  20.9 0.1 pad_maximum_fusion.2.x_all
  21.1 0.8 copy-done.7
  21.9 0.6 copy-done.14
  22.5 0.3 cosine_multiply_fusion.2
  22.9 0.3 broadcast_multiply_fusion.1
  23.2 14.2 %all-to-all-done.recv = f32[16,104,128]{2,1,0:T(8,128)S(1)} async-done(((f32[16,104,128]{2,1,0:T(8,128)}), f32[16,104,128]{2,1,0:T(8,128)S(1)}, u32[]{:S(2)}, u32[]{:S(2)}) %all-to-all-start) | async-done | bytes 852000 | tf_op jit(solution)/shard_map/all_to_all | solution.py:226
  37.4 21.2 %density.1 = (f32[800,128]{1,0:T(8,128)S(1)}, f32[800,128]{1,0:T(8,128)S(1)}) custom-call(f32[4]{0:T(128)S(1)} %multiply_bitcast_fusion.factors, f32[16,104,128]{2,1,0:T(8,128)S(1)} %all-to-all-done.recv, bf16[2,256,256]{2,1,0:T(8,128)(2,1)S(1)} %copy-done, bf16[2,128,256]{2,1,0:T(8,128)(2,1)S(1)} %copy-done.1, bf16[192,192]{1,0:T(8,128)(2,1)S(1)} %copy-done.2, ...), custom_call_target="tpu_custom_call" | custom-call | tf_op jit(solution)/shard_map/density/pallas_call | solution.py:237
  58.6 3.5 %collective-permute-start = (f32[800,128]{1,0:T(8,128)S(1)}, f32[800,128]{1,0:T(8,128)S(1)}, u32[]{:S(2)}, u32[]{:S(2)}) collective-permute-start(f32[800,128]{1,0:T(8,128)S(1)} %get-tuple-element.8), channel_id=1, source_target_pairs={{0,16},{16,0},{32,48},{48,32},{64,80},{80,64},{96,112},{112,96},{1... | collective-permute-start | bytes 1228808 | tf_op jit(solution)/shard_map/ppermute | solution.py:252
  62.3 0.1 reduce-precision_convert_fusion
  62.5 0.1 pad_maximum_fusion.1.atom_z
  62.6 0.9 collective-permute-done.arrived
  63.5 11.9 %force.1 = f32[16,8,128]{2,1,0:T(8,128)S(1)} custom-call(f32[32]{0:T(128)S(1)} %fusion.29.gx2, f32[800,128]{1,0:T(8,128)S(1)} %get-tuple-element.7.own, f32[800,128]{1,0:T(8,128)S(1)} %collective-permute-done.arrived, f32[96,128]{1,0:T(8,128)S(1)} %copy-done.4, bf16[192,48]{1,0:T(8,128)(2,1)S(1)} %pad_maximum_fusion.5.wave_z, ...), custom_call_target="tpu_custom_call" | custom-call | tf_op jit(solution)/shard_map/force/pallas_call | solution.py:293
  75.4 14.1 %all_to_all.15 = f32[16,8,128]{2,1,0:T(8,128)S(1)} all-to-all(f32[16,8,128]{2,1,0:T(8,128)S(1)} %force.1), channel_id=1, replica_groups=mesh['pool'=2,'band'=8,'fft'=16] {'pool','band'}, dimensions={0} | all-to-all | bytes 131072 | tf_op jit(solution)/shard_map/all_to_all | solution.py:305
  89.5 10.5 %all_to_all.16 = f32[16,8,128]{2,1,0:T(8,128)S(1)} all-to-all(f32[16,8,128]{2,1,0:T(8,128)S(1)} %broadcast_in_dim.125), channel_id=1, replica_groups=mesh['pool'=2,'band'=8,'fft'=16] {'fft'}, dimensions={0} | all-to-all | bytes 131072 | tf_op jit(solution)/shard_map/all_to_all | solution.py:307
  100.1 0.6 slice.15
  (53 shorter events, 1.0 us)
Async XLA Ops:
  0.0 0.7 copy-start.9
  2.6 1.0 copy-start.6
  5.4 32.0 %all-to-all-start = ((f32[16,104,128]{2,1,0:T(8,128)}), f32[16,104,128]{2,1,0:T(8,128)S(1)}, u32[]{:S(2)}, u32[]{:S(2)}) async-start(f32[16,104,128]{2,1,0:T(8,128)} %pad_maximum_fusion), calls=%async_computation | async-start | bytes 1703936 | tf_op jit(solution)/shard_map/all_to_all | solution.py:226
  15.7 0.7 copy-start.10
  15.7 0.7 copy-start.11
  15.7 0.7 copy-start.12
  16.6 0.7 copy-start.13
  19.9 0.7 copy-start.8
  20.9 0.9 copy-start.7
  21.9 0.7 copy-start.14
  21.9 15.5 %copy-start.3 = (bf16[256,128]{1,0:T(8,128)(2,1)S(1)}, bf16[256,128]{1,0:T(8,128)(2,1)}, u32[]{:S(2)}) copy-start(bf16[256,128]{1,0:T(8,128)(2,1)} %constant.149.clone.fwd_y1) | copy-start | bytes 196612
  22.5 14.9 %copy-start = (bf16[2,256,256]{2,1,0:T(8,128)(2,1)S(1)}, bf16[2,256,256]{2,1,0:T(8,128)(2,1)}, u32[]{:S(2)}) copy-start(bf16[2,256,256]{2,1,0:T(8,128)(2,1)} %constant.146.clone.inv_y1) | copy-start | bytes 786436
  22.9 14.5 %copy-start.1 = (bf16[2,128,256]{2,1,0:T(8,128)(2,1)S(1)}, bf16[2,128,256]{2,1,0:T(8,128)(2,1)}, u32[]{:S(2)}) copy-start(bf16[2,128,256]{2,1,0:T(8,128)(2,1)} %constant.147.clone.inv_y2) | copy-start | bytes 393220
  22.9 14.5 %copy-start.2 = (bf16[192,192]{1,0:T(8,128)(2,1)S(1)}, bf16[192,192]{1,0:T(8,128)(2,1)}, u32[]{:S(2)}) copy-start(bf16[192,192]{1,0:T(8,128)(2,1)} %constant.148.clone.inv_x) | copy-start | bytes 221188
  22.9 14.5 %copy-start.5 = (bf16[128,128]{1,0:T(8,128)(2,1)S(1)}, bf16[128,128]{1,0:T(8,128)(2,1)}, u32[]{:S(2)}) copy-start(bf16[128,128]{1,0:T(8,128)(2,1)} %constant.150.clone.fwd_y2) | copy-start | bytes 98308
  58.6 4.9 %collective-permute-start = (f32[800,128]{1,0:T(8,128)S(1)}, f32[800,128]{1,0:T(8,128)S(1)}, u32[]{:S(2)}, u32[]{:S(2)}) collective-permute-start(f32[800,128]{1,0:T(8,128)S(1)} %get-tuple-element.8), channel_id=1, source_target_pairs={{0,16},{16,0},{32,48},{48,32},{64,80},{80,64},{96,112},{112,96},{1... | collective-permute-start | bytes 1228808 | tf_op jit(solution)/shard_map/ppermute | solution.py:252
  62.5 1.0 %copy-start.4 = (f32[96,128]{1,0:T(8,128)S(1)}, f32[96,128]{1,0:T(8,128)}, u32[]{:S(2)}) copy-start(f32[96,128]{1,0:T(8,128)} %constant.151.clone.base) | copy-start | bytes 147460
where the time goes:
time: 101 us
  Pallas kernels  33 us (33%)
  blocking collectives  24.7 us (24%)
  waiting for transfers between devices  15 us (15%)
  starting transfers between devices  13.6 us (13%)
  local copies, waits for them, and re-layouts  7.31 us (7%)
  other arithmetic  4.04 us (4%)
  between operations  1.67 us (2%)
  matrix products  1.26 us (1%)
    pallas_call x1, Pallas kernels, shards(): pl.pallas_call(density_kernel, out_shape=(halves_shape, halves_shape), in...  21.2 us
    all_to_all x1, waiting for transfers between devices, shards(): lax.all_to_all(payload, 'fft', split_axis=0, concat_axis=0, tiled=True)  14.2 us
    all_to_all x1, blocking collectives, shards(): lax.all_to_all(spread, ('pool', 'band'), 0, 0, tiled=True)  14.1 us
    pallas_call x1, Pallas kernels, shards(): pl.pallas_call(force_kernel, out_shape=jax.ShapeDtypeStruct((16, 8, LANES...  11.9 us
    all_to_all x1, blocking collectives, shards(): total = jnp.sum(lax.all_to_all(spread, 'fft', 0, 0, tiled=True), axis=0)  10.5 us
    all_to_all x1, starting transfers between devices, shards(): lax.all_to_all(payload, 'fft', split_axis=0, concat_axis=0, tiled=True)  10.1 us
    unnamed x30, local copies, waits for them, and re-layouts  4.2 us
    ppermute x1, starting transfers between devices, shards(): arrived = lax.ppermute(other, 'band', swap)  3.51 us
  transfers between devices with their start and end apart: 2, of which 2 were waited for; matrix products, arithmetic and copies ran while one was open for 3% of the time, Pallas kernels for 0%

commit v1 on v0

--- a/solution.py
+++ b/solution.py
@@ -19,6 +19,8 @@
 PLANES = 12
 SLOTS = 25
 SIDE_ROWS = SLOTS * 16
+STICK_LIMIT = 113
+SPARE_ROW = SIDE * 64
 HIGH = lax.Precision.HIGH
 screen = 0.25
 VMEM = pl.BlockSpec(memory_space=pltpu.VMEM)
@@ -66,13 +68,12 @@
     both = np.zeros((SIDE, 256), np.float32)
     both[:, :96], both[:, 128:224] = cosine, sine
     high, low = np_halves(both)
-    first = np.zeros((2, 256, 256), high.dtype)
-    second = np.zeros((2, 128, 256), high.dtype)
+    table = np.zeros((2, 256, 256), high.dtype)
     for half in range(2):
         for part in range(2):
-            first[half, 128 * part + 64 * half : 128 * part + 64 * half + SIDE] = high
-        second[half, 64 * half : 64 * half + SIDE] = low
-    return first, second
+            table[half, 64 * part : 64 * part + SIDE] = high
+        table[half, 128 + 64 * half : 128 + 64 * half + SIDE] = low
+    return table
 
 
 def inverse_x_table():
@@ -106,36 +107,59 @@
 
 
 def density_kernel(
-    factors, recv, inv_y1, inv_y2, inv_x, fwd_y1, fwd_y2, fwd_x, own, other, parts, ids, held_re, held_im
+    factors,
+    recv,
+    inv_y,
+    inv_x,
+    fwd_y1,
+    fwd_y2,
+    fwd_x,
+    own,
+    other,
+    columns,
+    grid,
+    held_re,
+    held_im,
+    density,
+    ids_vector,
+    ids,
+    arrival,
 ):
     for source in range(16):
-        high, low = halves(recv[source, :96, :])
-        parts[:96, source * LANES : (source + 1) * LANES] = high
-        parts[96:, source * LANES : (source + 1) * LANES] = low
-        ids[:, source * LANES : (source + 1) * LANES] = recv[source, 96:104, :].astype(jnp.int32)
+        ids_vector[source : source + 1, :] = recv[source, 96:97, :].astype(jnp.int32)
+    to_scalars = pltpu.make_async_copy(ids_vector, ids, arrival)
+    to_scalars.start()
+    pad = jnp.zeros((32, LANES), jnp.float32)
+    for source in range(16):
+        columns[source] = jnp.concatenate([recv[source, :96, :], pad], 0).T
     blank = jnp.zeros((48, 128), jnp.float32)
     for row in range(52, 64):
         held_re[pl.ds(row, 48, stride=64), :] = blank
         held_im[pl.ds(row, 48, stride=64), :] = blank
+    grid[...] = jnp.zeros_like(grid)
+    to_scalars.wait()
+
+    def put(source, _):
+        for stick in range(STICK_LIMIT):
+            grid[pl.ds(ids[source, stick], 1), :] = columns[source, stick : stick + 1, :]
+        return 0
+
+    lax.fori_loop(0, 16, put, 0)
+    lower = lax.broadcasted_iota(jnp.int32, (96, 128), 1) < 64
 
     def place(tile, _):
-        cells = lax.broadcasted_iota(jnp.int32, (256, 256), 0) + tile * 256
-        total = jnp.zeros((192, 256), jnp.float32)
-        for block in range(8):
-            span = slice(block * 256, block * 256 + 256)
-            spots = (cells == ids[0:1, span]).astype(jnp.float32).astype(jnp.bfloat16)
-            total = total + lax.dot_general(
-                parts[:, span], spots, (((1,), (1,)), ((), ())), preferred_element_type=jnp.float32
-            )
-        grid = total[:96] + total[96:]
-        high, low = halves(grid)
-        for column in range(4):
-            pair = slice((column // 2) * 128, (column // 2) * 128 + 128)
-            both = jnp.concatenate([high[:, pair], low[:, pair]], 1)
-            out = mm(both, inv_y1[column % 2]) + mm(high[:, pair], inv_y2[column % 2])
-            rows = pl.ds(tile * 4 + column, 48, stride=64)
-            held_re[rows, :] = out[:48, :128] - out[48:, 128:]
-            held_im[rows, :] = out[48:, :128] + out[:48, 128:]
+        for pair in range(2):
+            start = pl.multiple_of(tile * 256 + pair * 128, 128)
+            rows = grid[pl.ds(start, 128), :].T[:96]
+            high = rows.astype(jnp.bfloat16).astype(jnp.float32)
+            low = pltpu.roll(rows - high, 64, 1)
+            for half in range(2):
+                mixed = jnp.where(lower, low, high) if half else jnp.where(lower, high, low)
+                both = jnp.concatenate([mixed, high], 1).astype(jnp.bfloat16)
+                out = mm(both, inv_y[half])
+                rows_to = pl.ds(tile * 4 + pair * 2 + half, 48, stride=64)
+                held_re[rows_to, :] = out[:48, :128] - out[48:, 128:]
+                held_im[rows_to, :] = out[48:, :128] + out[:48, 128:]
         return 0
 
     lax.fori_loop(0, 13, place, 0)
@@ -144,8 +168,8 @@
         own[pl.ds(row, 2 * SLOTS, stride=16), :] = clear
         other[pl.ds(row, 2 * SLOTS, stride=16), :] = clear
 
-    def plane_step(plane, _):
-        density = jnp.zeros((96, 128), jnp.float32)
+    def waves(plane, _):
+        total = jnp.zeros((96, 128), jnp.float32)
         for band in range(4):
             start = pl.multiple_of((band * PLANES + plane) * 64, 64)
             rows = pl.ds(start, 64)
@@ -153,19 +177,34 @@
             out = mm(inv_x[...], jnp.concatenate([high, low, high], 0))
             wave_re = out[:96, :128] - out[96:, 128:]
             wave_im = out[96:, :128] + out[:96, 128:]
-            density = density + factors[band] * (wave_re * wave_re + wave_im * wave_im)
-        high, low = halves(density)
+            total = total + factors[band] * (wave_re * wave_re + wave_im * wave_im)
+        density[pl.ds(pl.multiple_of(plane * 96, 96), 96), :] = total
+        return 0
+
+    lax.fori_loop(0, PLANES, waves, 0, unroll=2)
+
+    def forward(group, _):
+        start = pl.multiple_of(group * 384, 384)
+        high, low = halves(density[pl.ds(start, 384), :])
         rows = mm(jnp.concatenate([high, low], 1), fwd_y1[...]) + mm(high, fwd_y2[...])
         high, low = halves(rows)
-        out = mm(fwd_x[...], jnp.concatenate([high, low, high], 0))
-        first, second = pl.ds(plane, SLOTS, stride=16), pl.ds(plane + SIDE_ROWS, SLOTS, stride=16)
-        own[first, :] = out[0:SLOTS]
-        own[second, :] = out[32 : 32 + SLOTS]
-        other[first, :] = out[64 : 64 + SLOTS]
-        other[second, :] = out[96 : 96 + SLOTS]
-        return 0
-
-    lax.fori_loop(0, PLANES, plane_step, 0)
+        for pair in range(2):
+            first, second = slice(pair * 192, pair * 192 + 96), slice(pair * 192 + 96, pair * 192 + 192)
+            wide_high = jnp.concatenate([high[first], high[second]], 1)
+            wide_low = jnp.concatenate([low[first], low[second]], 1)
+            out = mm(fwd_x[...], jnp.concatenate([wide_high, wide_low, wide_high], 0))
+            for member in range(2):
+                plane = group * 4 + pair * 2 + member
+                lanes = slice(member * 128, member * 128 + 128)
+                cosine = pl.ds(plane, SLOTS, stride=16)
+                sine = pl.ds(plane + SIDE_ROWS, SLOTS, stride=16)
+                own[cosine, :] = out[0:SLOTS, lanes]
+                own[sine, :] = out[32 : 32 + SLOTS, lanes]
+                other[cosine, :] = out[64 : 64 + SLOTS, lanes]
+                other[sine, :] = out[96 : 96 + SLOTS, lanes]
+        return 0
+
+    lax.fori_loop(0, 3, forward, 0)
 
 
 def force_kernel(gx2, own, arrived, base, wave_z, atom_z, x_all, y_cos, y_sin, strength, out, acc, turn):
@@ -193,7 +232,7 @@
         turn[...] = pltpu.roll(table, 127, 1)
         return 0
 
-    lax.fori_loop(0, SLOTS, step, 0)
+    lax.fori_loop(0, SLOTS, step, 0, unroll=5)
     parts = [acc[0] * y_cos[...], acc[1] * y_sin[...], acc[2] * y_cos[...]]
     rows = [-strength[...] * jnp.sum(part.T, axis=0, keepdims=True) for part in parts]
     block = jnp.concatenate(rows + [jnp.zeros((5, 128), jnp.float32)], 0)
@@ -217,8 +256,8 @@
     rank = jnp.sum(jnp.where(before & chosen[:, None], 1, 0), axis=0)
     lane = jnp.arange(LANES, dtype=jnp.int32)
     pick = (chosen[:, None] & (rank[:, None] == lane[None, :])).astype(jnp.float32)
-    place = ((freq_x + HALF) * 64 + freq_y + HALF + 1).astype(jnp.float32)
-    ids = jnp.sum(pick * place[:, None], axis=0) - 1.0
+    place = ((freq_x + HALF) * 64 + freq_y + HALF - SPARE_ROW).astype(jnp.float32)
+    ids = jnp.sum(pick * place[:, None], axis=0) + float(SPARE_ROW)
     packed = jnp.einsum("bcst,sj->bctj", masked, pick, precision=HIGH)
     planes = jnp.einsum("dpoct,bctj->dobpj", z_table(), packed, precision=HIGH)
     planes = planes.reshape(16, 96, LANES)
@@ -230,24 +269,27 @@
         kpoint_weight, lax.axis_index("pool"), keepdims=False
     ).astype(jnp.float32) / jnp.sum(kpoint_weight).astype(jnp.float32)
     factors = pool_weight * occupation[0] * (16.0 / NGRID / 32.0 / NGRID)
-    inv_y1, inv_y2 = inverse_y_tables()
     fwd_y1, fwd_y2 = forward_y_tables()
     fwd_x = lax.dynamic_index_in_dim(jnp.asarray(forward_x_tables()), core, keepdims=False)
     halves_shape = jax.ShapeDtypeStruct((2 * SIDE_ROWS, 128), jnp.float32)
     own, other = pl.pallas_call(
         density_kernel,
         out_shape=(halves_shape, halves_shape),
-        in_specs=[SMEM] + [VMEM] * 7,
+        in_specs=[SMEM] + [VMEM] * 6,
         out_specs=(VMEM, VMEM),
         scratch_shapes=[
-            pltpu.VMEM((192, 2048), jnp.bfloat16),
-            pltpu.VMEM((8, 2048), jnp.int32),
-            pltpu.VMEM((48 * 64, 128), jnp.float32),
-            pltpu.VMEM((48 * 64, 128), jnp.float32),
+            pltpu.VMEM((16, LANES, LANES), jnp.float32),
+            pltpu.VMEM((52 * 64, LANES), jnp.float32),
+            pltpu.VMEM((48 * 64, LANES), jnp.float32),
+            pltpu.VMEM((48 * 64, LANES), jnp.float32),
+            pltpu.VMEM((PLANES * 96, LANES), jnp.float32),
+            pltpu.VMEM((16, LANES), jnp.int32),
+            pltpu.SMEM((16, LANES), jnp.int32),
+            pltpu.SemaphoreType.DMA,
         ],
         compiler_params=pltpu.CompilerParams(vmem_limit_bytes=40 * 1024 * 1024),
         name="density",
-    )(factors, received, inv_y1, inv_y2, inverse_x_table(), fwd_y1, fwd_y2, fwd_x)
+    )(factors, received, inverse_y_tables(), inverse_x_table(), fwd_y1, fwd_y2, fwd_x)
     swap = [(index, index ^ 1) for index in range(8)]
     arrived = lax.ppermute(other, "band", swap)
 

time: 101 us -> 88.7 us (0.88)
  Pallas kernels: 33 us -> 20.7 us
    pallas_call x1, Pallas kernels: 21.2 us -> 13.7 us  [shards(): pl.pallas_call(density_kernel, out_shape=(halves_shape, halves_shape), in...]
    pallas_call x1, Pallas kernels: 11.9 us -> 6.95 us  [shards(): pl.pallas_call(force_kernel, out_shape=jax.ShapeDtypeStruct((16, 8, LANES...]
    unnamed x30 -> x28, local copies, waits for them, and re-layouts: 4.2 us -> 4.2 us
  transfers between devices with their start and end apart: 2 -> 2, of which waited for: 2 -> 2; matrix products, arithmetic and copies ran while one was open for 3% -> 4% of each run, Pallas kernels for 0% -> 0%
where the time goes in v1:
time: 88.7 us; the launch traced here: 88.3 us
  blocking collectives  24.7 us (28%)
  Pallas kernels  20.7 us (23%)
  waiting for transfers between devices  15.1 us (17%)
  starting transfers between devices  13.6 us (15%)
  local copies, waits for them, and re-layouts  7.3 us (8%)
  other arithmetic  4.02 us (5%)
  between operations  1.59 us (2%)
  matrix products  1.26 us (1%)
    all_to_all x1, waiting for transfers between devices, shards(): lax.all_to_all(payload, 'fft', split_axis=0, concat_axis=0, tiled=True)  14.3 us
    all_to_all x1, blocking collectives, shards(): lax.all_to_all(spread, ('pool', 'band'), 0, 0, tiled=True)  14.1 us
    pallas_call x1, Pallas kernels, shards(): pl.pallas_call(density_kernel, out_shape=(halves_shape, halves_shape), in...  13.7 us
    all_to_all x1, blocking collectives, shards(): total = jnp.sum(lax.all_to_all(spread, 'fft', 0, 0, tiled=True), axis=0)  10.5 us
    all_to_all x1, starting transfers between devices, shards(): lax.all_to_all(payload, 'fft', split_axis=0, concat_axis=0, tiled=True)  10.1 us
    pallas_call x1, Pallas kernels, shards(): pl.pallas_call(force_kernel, out_shape=jax.ShapeDtypeStruct((16, 8, LANES...  6.95 us
    unnamed x28, local copies, waits for them, and re-layouts  4.2 us
    ppermute x1, starting transfers between devices, shards(): arrived = lax.ppermute(other, 'band', swap)  3.5 us
  transfers between devices with their start and end apart: 2, of which 2 were waited for; matrix products, arithmetic and copies ran while one was open for 4% of the time, Pallas kernels for 0%

profile of v1, /device:TPU:1, one launch (start us, length us, event | category | flops | bytes accessed | tf_op | source)
XLA Modules:
  0.0 88.3 jit_solution(1834425037794423229)
XLA Ops:
  0.0 0.7 copy-done.8
  0.8 0.1 select_reduce_fusion.1
  1.0 1.5 %reshape_squeeze.3 = f32[4,2,144,96]{3,2,1,0:T(8,128)S(1)} reshape(f32[1,4,2,13824]{3,2,1,0:T(2,128)} %param.15) | data formatting | bytes 884736 | tf_op jit(solution)/shard_map/reshape;squeeze | solution.py:247
  2.6 0.7 convolution_bitcast_fusion.1
  3.3 0.2 copy-done.5
  3.6 0.5 convolution_bitcast_fusion
  4.2 0.3 copy.26
  4.4 1.0 %pad_maximum_fusion = f32[16,104,128]{2,1,0:T(8,128)} fusion(f32[16,8,128]{2,1,0:T(8,128)S(1)} %broadcast_in_dim.113, f32[16,96,128]{2,1,0:T(8,128)S(1)} %copy.26), kind=kLoop, calls=%fused_computation.2 | loop fusion | flops 212992 | bytes 1703936 | tf_op jit(solution)/shard_map/concatenate | solution.py:264
  5.4 10.1 %all-to-all-start = ((f32[16,104,128]{2,1,0:T(8,128)}), f32[16,104,128]{2,1,0:T(8,128)S(1)}, u32[]{:S(2)}, u32[]{:S(2)}) async-start(f32[16,104,128]{2,1,0:T(8,128)} %pad_maximum_fusion), calls=%async_computation | async-start | bytes 1703936 | tf_op jit(solution)/shard_map/all_to_all | solution.py:265
  15.7 0.1 fusion.19
  15.9 0.5 copy-done.9
  16.6 0.7 copy-done.12
  17.2 0.6 reduce_sum.63
  17.9 0.6 dynamic_slice.8
  19.7 0.1 copy.27
  19.8 0.7 copy-done.7
  20.5 0.3 cosine_multiply_fusion.1
  20.9 0.1 pad_maximum_fusion.2.x_all
  21.0 0.8 copy-done.6
  21.8 0.6 copy-done.13
  22.4 0.3 cosine_multiply_fusion.2
  22.8 0.3 broadcast_multiply_fusion.1
  23.1 14.3 %all-to-all-done.recv = f32[16,104,128]{2,1,0:T(8,128)S(1)} async-done(((f32[16,104,128]{2,1,0:T(8,128)}), f32[16,104,128]{2,1,0:T(8,128)S(1)}, u32[]{:S(2)}, u32[]{:S(2)}) %all-to-all-start) | async-done | bytes 852000 | tf_op jit(solution)/shard_map/all_to_all | solution.py:265
  37.4 13.7 %density.1 = (f32[800,128]{1,0:T(8,128)S(1)}, f32[800,128]{1,0:T(8,128)S(1)}) custom-call(f32[4]{0:T(128)S(1)} %multiply_bitcast_fusion.factors, f32[16,104,128]{2,1,0:T(8,128)S(1)} %all-to-all-done.recv, bf16[2,256,256]{2,1,0:T(8,128)(2,1)S(1)} %copy-done, bf16[192,192]{1,0:T(8,128)(2,1)S(1)} %copy-done.1, bf16[256,128]{1,0:T(8,128)(2,1)S(1)} %copy-done.2, ...), custom_call_target="tpu_custom_call" | custom-call | tf_op jit(solution)/shard_map/density/pallas_call | solution.py:275
  51.1 3.5 %collective-permute-start = (f32[800,128]{1,0:T(8,128)S(1)}, f32[800,128]{1,0:T(8,128)S(1)}, u32[]{:S(2)}, u32[]{:S(2)}) collective-permute-start(f32[800,128]{1,0:T(8,128)S(1)} %get-tuple-element.8), channel_id=1, source_target_pairs={{0,16},{16,0},{32,48},{48,32},{64,80},{80,64},{96,112},{112,96},{1... | collective-permute-start | bytes 1228808 | tf_op jit(solution)/shard_map/ppermute | solution.py:294
  54.8 0.1 reduce-precision_convert_fusion
  55.0 0.1 pad_maximum_fusion.1.atom_z
  55.1 0.9 collective-permute-done.arrived
  56.0 7.0 %force.1 = f32[16,8,128]{2,1,0:T(8,128)S(1)} custom-call(f32[32]{0:T(128)S(1)} %fusion.29.gx2, f32[800,128]{1,0:T(8,128)S(1)} %get-tuple-element.7.own, f32[800,128]{1,0:T(8,128)S(1)} %collective-permute-done.arrived, f32[96,128]{1,0:T(8,128)S(1)} %copy-done.3, bf16[192,48]{1,0:T(8,128)(2,1)S(1)} %pad_maximum_fusion.5.wave_z, ...), custom_call_target="tpu_custom_call" | custom-call | tf_op jit(solution)/shard_map/force/pallas_call | solution.py:335
  63.0 14.1 %all_to_all.15 = f32[16,8,128]{2,1,0:T(8,128)S(1)} all-to-all(f32[16,8,128]{2,1,0:T(8,128)S(1)} %force.1), channel_id=1, replica_groups=mesh['pool'=2,'band'=8,'fft'=16] {'pool','band'}, dimensions={0} | all-to-all | bytes 131072 | tf_op jit(solution)/shard_map/all_to_all | solution.py:347
  77.1 10.5 %all_to_all.16 = f32[16,8,128]{2,1,0:T(8,128)S(1)} all-to-all(f32[16,8,128]{2,1,0:T(8,128)S(1)} %broadcast_in_dim.125), channel_id=1, replica_groups=mesh['pool'=2,'band'=8,'fft'=16] {'fft'}, dimensions={0} | all-to-all | bytes 131072 | tf_op jit(solution)/shard_map/all_to_all | solution.py:349
  87.7 0.6 slice.15
  (51 shorter events, 1.0 us)
Async XLA Ops:
  0.0 0.7 copy-start.8
  2.6 1.0 %copy-start.5 = (f32[16,12,2,2,96,1]{4,0,3,2,1,5:T(8,128)S(1)}, f32[16,12,2,2,96,1]{4,0,3,2,1,5:T(8,128)}, u32[]{:S(2)}) copy-start(f32[16,12,2,2,96,1]{4,0,3,2,1,5:T(8,128)} %constant.153) | copy-start | bytes 884740
  5.4 32.0 %all-to-all-start = ((f32[16,104,128]{2,1,0:T(8,128)}), f32[16,104,128]{2,1,0:T(8,128)S(1)}, u32[]{:S(2)}, u32[]{:S(2)}) async-start(f32[16,104,128]{2,1,0:T(8,128)} %pad_maximum_fusion), calls=%async_computation | async-start | bytes 1703936 | tf_op jit(solution)/shard_map/all_to_all | solution.py:265
  15.7 0.7 copy-start.9
  15.7 0.7 copy-start.10
  15.7 0.7 copy-start.11
  16.6 0.7 copy-start.12
  19.8 0.7 copy-start.7
  20.8 0.9 %copy-start.6 = (bf16[2,128,288]{2,1,0:T(8,128)(2,1)S(1)}, bf16[2,128,288]{2,1,0:T(8,128)(2,1)}, u32[]{:S(2)}) copy-start(bf16[2,128,288]{2,1,0:T(8,128)(2,1)} %constant.143.clone) | copy-start | bytes 442372
  21.8 0.7 copy-start.13
  22.4 15.0 %copy-start = (bf16[2,256,256]{2,1,0:T(8,128)(2,1)S(1)}, bf16[2,256,256]{2,1,0:T(8,128)(2,1)}, u32[]{:S(2)}) copy-start(bf16[2,256,256]{2,1,0:T(8,128)(2,1)} %constant.144.clone.inv_y) | copy-start | bytes 786436
  22.8 14.6 %copy-start.1 = (bf16[192,192]{1,0:T(8,128)(2,1)S(1)}, bf16[192,192]{1,0:T(8,128)(2,1)}, u32[]{:S(2)}) copy-start(bf16[192,192]{1,0:T(8,128)(2,1)} %constant.145.clone.inv_x) | copy-start | bytes 221188
  22.8 14.6 %copy-start.2 = (bf16[256,128]{1,0:T(8,128)(2,1)S(1)}, bf16[256,128]{1,0:T(8,128)(2,1)}, u32[]{:S(2)}) copy-start(bf16[256,128]{1,0:T(8,128)(2,1)} %constant.146.clone.fwd_y1) | copy-start | bytes 196612
  22.8 14.6 %copy-start.4 = (bf16[128,128]{1,0:T(8,128)(2,1)S(1)}, bf16[128,128]{1,0:T(8,128)(2,1)}, u32[]{:S(2)}) copy-start(bf16[128,128]{1,0:T(8,128)(2,1)} %constant.147.clone.fwd_y2) | copy-start | bytes 98308
  51.1 4.9 %collective-permute-start = (f32[800,128]{1,0:T(8,128)S(1)}, f32[800,128]{1,0:T(8,128)S(1)}, u32[]{:S(2)}, u32[]{:S(2)}) collective-permute-start(f32[800,128]{1,0:T(8,128)S(1)} %get-tuple-element.8), channel_id=1, source_target_pairs={{0,16},{16,0},{32,48},{48,32},{64,80},{80,64},{96,112},{112,96},{1... | collective-permute-start | bytes 1228808 | tf_op jit(solution)/shard_map/ppermute | solution.py:294
  55.0 1.0 %copy-start.3 = (f32[96,128]{1,0:T(8,128)S(1)}, f32[96,128]{1,0:T(8,128)}, u32[]{:S(2)}) copy-start(f32[96,128]{1,0:T(8,128)} %constant.148.clone.base) | copy-start | bytes 147460

commit v2 on v1

--- a/solution.py
+++ b/solution.py
@@ -20,9 +20,15 @@
 SLOTS = 25
 SIDE_ROWS = SLOTS * 16
 STICK_LIMIT = 113
+SPARE = 15
+ROWS = 88
+NEAR = 80
+HELD = 72
+GROUPS = 36
 SPARE_ROW = SIDE * 64
 HIGH = lax.Precision.HIGH
 screen = 0.25
+AXES = ("pool", "band", "fft")
 VMEM = pl.BlockSpec(memory_space=pltpu.VMEM)
 SMEM = pl.BlockSpec(memory_space=pltpu.SMEM)
 
@@ -36,6 +42,13 @@
     return np.cos(angles).astype(np.float32), np.sin(angles).astype(np.float32)
 
 
+def reduce_groups():
+    ranks = np.arange(256).reshape(2, 4, 2, 8, 2)
+    across = ranks.transpose(3, 2, 0, 4, 1).reshape(16, 16)
+    along = ranks.transpose(0, 4, 1, 3, 2).reshape(16, 16)
+    return across.tolist(), along.tolist()
+
+
 def halves(values):
     high = values.astype(jnp.bfloat16)
     return high, (values - high.astype(jnp.float32)).astype(jnp.bfloat16)
@@ -56,11 +69,9 @@
 
 
 def z_table():
-    cosine, sine = trig(np.arange(NZ), np.arange(ZSPAN) - NZ // 4, NZ)
-    real_rows = np.stack([cosine, -sine], 1)
-    imag_rows = np.stack([sine, cosine], 1)
-    table = np.stack([real_rows, imag_rows], 1)
-    return table.reshape(16, PLANES, 2, 2, ZSPAN)
+    both = np.zeros((2, NZ, LANES), np.float32)
+    both[:, :, :ZSPAN] = trig(np.arange(NZ), np.arange(ZSPAN) - NZ // 4, NZ)
+    return np.concatenate(np_halves(both.reshape(2 * NZ, LANES)), 1)
 
 
 def inverse_y_tables():
@@ -104,6 +115,72 @@
         high, low = np_halves(both)
         result.append(np.concatenate([high, high, low], 1))
     return np.stack(result)
+
+
+def mm_t(left, right):
+    return lax.dot_general(
+        left, right, (((1,), (1,)), ((), ())), preferred_element_type=jnp.float32
+    )
+
+
+def pieces(held, dest, tile):
+    found = []
+    for row in range(tile * 8, tile * 8 + 8, 4):
+        start = (row // 48) * 192 + dest * PLANES + row % 12
+        found.append(held[(row % 48) // 12, start : start + 4, :])
+    return jnp.concatenate(found, 0)
+
+
+def send_kernel(coefs, mask, pick, ids, table, out, held, rows):
+    for chunk in range(3 * GROUPS):
+        piece = coefs[:, :, chunk * LANES : (chunk + 1) * LANES]
+        for band in range(4):
+            for part in range(2):
+                start = (band * 2 + part) * 40 + chunk // 3
+                rows[chunk % 3, start : start + 1, :] = piece[band, part : part + 1]
+    high_table = table[:, :LANES]
+    wide_table = jnp.concatenate([high_table, high_table], 1)
+    low_table = table[:, LANES:]
+    low_lane = lax.broadcasted_iota(jnp.int32, (40, LANES), 1)
+    filler = jnp.zeros((96, 256), jnp.bfloat16)
+    for band in range(4):
+        highs, lows = [], []
+        for part in range(2):
+            span = slice((band * 2 + part) * 40, (band * 2 + part) * 40 + 40)
+            first, second, third = rows[0, span, :], rows[1, span, :], rows[2, span, :]
+            quarters = [
+                first,
+                jnp.where(low_lane < 32, pltpu.roll(first, 32, 1), pltpu.roll(second, 32, 1)),
+                jnp.where(low_lane < 64, pltpu.roll(second, 64, 1), pltpu.roll(third, 64, 1)),
+                pltpu.roll(third, 96, 1),
+            ]
+            values = jnp.concatenate(quarters, 0)
+            values = jnp.where(mask[...] > 0.0, values, 0.0)
+            both = jnp.concatenate(halves(values), 1)
+            chosen = mm(pick[...], jnp.concatenate([both, filler], 0))
+            highs.append(chosen[:, :128].astype(jnp.bfloat16))
+            lows.append(chosen[:, 128:].astype(jnp.bfloat16))
+        high = jnp.concatenate(highs, 0)
+        spread = jnp.concatenate([high, jnp.concatenate(lows, 0)], 1)
+        waves = mm_t(wide_table, spread) + mm_t(low_table, high)
+        cosine, sine = waves[:192], waves[192:]
+        held[band, :192] = cosine[:, :128] - sine[:, 128:]
+        held[band, 192:] = sine[:, :128] + cosine[:, 128:]
+    lane = lax.broadcasted_iota(jnp.int32, (8, LANES), 1)
+    row = lax.broadcasted_iota(jnp.int32, (8, LANES), 0)
+    marks = jnp.zeros((8, LANES), jnp.float32)
+    spots = jnp.broadcast_to(ids[...], (8, LANES))
+    for index in range(8):
+        marks = jnp.where(row == index, pltpu.roll(spots, STICK_LIMIT - SPARE * index, 1), marks)
+    for dest in range(16):
+        tail = pieces(held, dest, 11)
+        for tile in range(11):
+            main = pieces(held, dest, tile)
+            if tile < 8:
+                extra = pltpu.roll(tail, STICK_LIMIT - SPARE * tile, 1)
+            else:
+                extra = marks
+            out[dest, tile * 8 : tile * 8 + 8, :] = jnp.where(lane < STICK_LIMIT, main, extra)
 
 
 def density_kernel(
@@ -125,17 +202,27 @@
     ids,
     arrival,
 ):
-    for source in range(16):
-        ids_vector[source : source + 1, :] = recv[source, 96:97, :].astype(jnp.int32)
+    lane = lax.broadcasted_iota(jnp.int32, (16, LANES), 1)
+    marks = jnp.zeros((16, LANES), jnp.float32)
+    for index in range(8):
+        rolled = pltpu.roll(recv[pl.ds(64 + index, 16, stride=ROWS), :], 15 + SPARE * index, 1)
+        marks = jnp.where(lane // SPARE == index, rolled, marks)
+    ids_vector[...] = marks.astype(jnp.int32)
     to_scalars = pltpu.make_async_copy(ids_vector, ids, arrival)
     to_scalars.start()
+    lane = lane[:8]
     pad = jnp.zeros((32, LANES), jnp.float32)
     for source in range(16):
-        columns[source] = jnp.concatenate([recv[source, :96, :], pad], 0).T
+        first = source * ROWS
+        tail = jnp.zeros((8, LANES), jnp.float32)
+        for tile in range(8):
+            piece = recv[first + tile * 8 : first + tile * 8 + 8, :]
+            tail = jnp.where(lane // SPARE == tile, pltpu.roll(piece, 15 + SPARE * tile, 1), tail)
+        columns[source] = jnp.concatenate([recv[first : first + ROWS, :], tail, pad], 0).T
     blank = jnp.zeros((48, 128), jnp.float32)
-    for row in range(52, 64):
-        held_re[pl.ds(row, 48, stride=64), :] = blank
-        held_im[pl.ds(row, 48, stride=64), :] = blank
+    for row in range(50, 64):
+        held_re[pl.ds(row, 48, stride=HELD), :] = blank
+        held_im[pl.ds(row, 48, stride=HELD), :] = blank
     grid[...] = jnp.zeros_like(grid)
     to_scalars.wait()
 
@@ -147,22 +234,20 @@
     lax.fori_loop(0, 16, put, 0)
     lower = lax.broadcasted_iota(jnp.int32, (96, 128), 1) < 64
 
-    def place(tile, _):
-        for pair in range(2):
-            start = pl.multiple_of(tile * 256 + pair * 128, 128)
-            rows = grid[pl.ds(start, 128), :].T[:96]
-            high = rows.astype(jnp.bfloat16).astype(jnp.float32)
-            low = pltpu.roll(rows - high, 64, 1)
-            for half in range(2):
-                mixed = jnp.where(lower, low, high) if half else jnp.where(lower, high, low)
-                both = jnp.concatenate([mixed, high], 1).astype(jnp.bfloat16)
-                out = mm(both, inv_y[half])
-                rows_to = pl.ds(tile * 4 + pair * 2 + half, 48, stride=64)
-                held_re[rows_to, :] = out[:48, :128] - out[48:, 128:]
-                held_im[rows_to, :] = out[48:, :128] + out[:48, 128:]
+    def place(pair, _):
+        rows = grid[pl.ds(pl.multiple_of(pair * 128, 128), 128), :].T[:96]
+        high = rows.astype(jnp.bfloat16).astype(jnp.float32)
+        low = pltpu.roll(rows - high, 64, 1)
+        for half in range(2):
+            mixed = jnp.where(lower, low, high) if half else jnp.where(lower, high, low)
+            both = jnp.concatenate([mixed, high], 1).astype(jnp.bfloat16)
+            out = mm(both, inv_y[half])
+            rows_to = pl.ds(pair * 2 + half, 48, stride=HELD)
+            held_re[rows_to, :] = out[:48, :128] - out[48:, 128:]
+            held_im[rows_to, :] = out[48:, :128] + out[:48, 128:]
         return 0
 
-    lax.fori_loop(0, 13, place, 0)
+    lax.fori_loop(0, 25, place, 0, unroll=25)
     clear = jnp.zeros((2 * SLOTS, 128), jnp.float32)
     for row in range(PLANES, 16):
         own[pl.ds(row, 2 * SLOTS, stride=16), :] = clear
@@ -171,7 +256,7 @@
     def waves(plane, _):
         total = jnp.zeros((96, 128), jnp.float32)
         for band in range(4):
-            start = pl.multiple_of((band * PLANES + plane) * 64, 64)
+            start = pl.multiple_of((band * PLANES + plane) * HELD, HELD)
             rows = pl.ds(start, 64)
             high, low = halves(jnp.concatenate([held_re[rows, :], held_im[rows, :]], 1))
             out = mm(inv_x[...], jnp.concatenate([high, low, high], 0))
@@ -181,7 +266,7 @@
         density[pl.ds(pl.multiple_of(plane * 96, 96), 96), :] = total
         return 0
 
-    lax.fori_loop(0, PLANES, waves, 0, unroll=2)
+    lax.fori_loop(0, PLANES, waves, 0, unroll=4)
 
     def forward(group, _):
         start = pl.multiple_of(group * 384, 384)
@@ -204,24 +289,29 @@
                 other[sine, :] = out[96 : 96 + SLOTS, lanes]
         return 0
 
-    lax.fori_loop(0, 3, forward, 0)
-
-
-def force_kernel(gx2, own, arrived, base, wave_z, atom_z, x_all, y_cos, y_sin, strength, out, acc, turn):
+    lax.fori_loop(0, 3, forward, 0, unroll=3)
+
+
+def force_kernel(
+    gx2, own, arrived, base, wave_z, atom_z, near_z, x_all, y_cos, y_sin, strength, out, acc, turn
+):
     acc[...] = jnp.zeros_like(acc)
     turn[...] = x_all[...]
 
-    def step(slot, _):
+    def step(slot, reach, phases):
         start = pl.multiple_of(slot * 16, 16)
         first, second = pl.ds(start, 16), pl.ds(start + SIDE_ROWS, 16)
         pair = [own[first, :] + arrived[first, :], own[second, :] + arrived[second, :]]
         high, low = halves(jnp.concatenate(pair, 1))
-        raw = mm(wave_z[...], jnp.concatenate([high, low, high], 0))
-        weight = 1.0 / (base[...] + gx2[slot])
+        waves = wave_z[...]
+        if reach < ZSPAN:
+            waves = jnp.concatenate([waves[:reach], waves[ZSPAN : ZSPAN + reach]], 0)
+        raw = mm(waves, jnp.concatenate([high, low, high], 0))
+        weight = 1.0 / (base[:reach] + gx2[slot])
         weight = jnp.concatenate([weight, weight], 1)
         weight = jnp.concatenate([weight, weight], 0)
         high, low = halves(raw * weight)
-        both = mm(atom_z[...], jnp.concatenate([high, low, high], 0))
+        both = mm(phases[...], jnp.concatenate([high, low, high], 0))
         table = turn[...]
         xc_c, xc_s = table[:, 0:1], table[:, 32:33]
         xs_c, xs_s = table[:, 64:65], table[:, 96:97]
@@ -232,10 +322,11 @@
         turn[...] = pltpu.roll(table, 127, 1)
         return 0
 
-    lax.fori_loop(0, SLOTS, step, 0, unroll=5)
+    lax.fori_loop(0, 14, lambda slot, _: step(slot, ZSPAN, atom_z), 0, unroll=7)
+    lax.fori_loop(14, SLOTS, lambda slot, _: step(slot, NEAR, near_z), 0, unroll=11)
     parts = [acc[0] * y_cos[...], acc[1] * y_sin[...], acc[2] * y_cos[...]]
     rows = [-strength[...] * jnp.sum(part.T, axis=0, keepdims=True) for part in parts]
-    block = jnp.concatenate(rows + [jnp.zeros((5, 128), jnp.float32)], 0)
+    block = jnp.concatenate(rows, 0)
     for index in range(16):
         out[index] = block
 
@@ -243,26 +334,36 @@
 def shards(
     coefficients, occupation, kpoint_weight, stick_cell, species, positions, amplitude, core_width
 ):
-    sticks = stick_cell.shape[0]
-    shaped = coefficients[0].reshape(4, 2, sticks, ZSPAN)
-    freq_x = signed_freq(stick_cell // NY, NX)
-    freq_y = signed_freq(stick_cell % NY, NY)
-    freq_z = jnp.arange(ZSPAN, dtype=jnp.int32) - NZ // 4
+    cells = jnp.pad(stick_cell.reshape(GROUPS, 4).T, ((0, 0), (0, 4)), constant_values=48 * NY)
+    cells = cells.reshape(160)
+    freq_x = signed_freq(cells // NY, NX)
+    freq_y = signed_freq(cells % NY, NY)
+    freq_z = jnp.arange(LANES, dtype=jnp.int32) - NZ // 4
     disk = 16 * (freq_x * freq_x + freq_y * freq_y)
     level = disk[:, None] + 4 * (freq_z * freq_z)[None, :]
-    masked = jnp.where(level <= NX * NX, shaped, 0.0)
+    mask = ((level <= NX * NX) & (freq_z < NZ // 4)[None, :]).astype(jnp.float32)
     chosen = disk <= NX * NX
-    before = jnp.arange(sticks)[:, None] < jnp.arange(sticks)[None, :]
+    before = jnp.arange(160)[:, None] < jnp.arange(160)[None, :]
     rank = jnp.sum(jnp.where(before & chosen[:, None], 1, 0), axis=0)
     lane = jnp.arange(LANES, dtype=jnp.int32)
-    pick = (chosen[:, None] & (rank[:, None] == lane[None, :])).astype(jnp.float32)
-    place = ((freq_x + HALF) * 64 + freq_y + HALF - SPARE_ROW).astype(jnp.float32)
-    ids = jnp.sum(pick * place[:, None], axis=0) + float(SPARE_ROW)
-    packed = jnp.einsum("bcst,sj->bctj", masked, pick, precision=HIGH)
-    planes = jnp.einsum("dpoct,bctj->dobpj", z_table(), packed, precision=HIGH)
-    planes = planes.reshape(16, 96, LANES)
-    payload = jnp.concatenate([planes, jnp.broadcast_to(ids[None, None], (16, 8, LANES))], 1)
+    pick = chosen[None, :] & (rank[None, :] == lane[:, None])
+    place = (freq_x + HALF) * 64 + freq_y + HALF
+    ids = jnp.sum(jnp.where(pick, place[None, :] - SPARE_ROW, 0), axis=1) + SPARE_ROW
+    pick = jnp.pad(pick.astype(jnp.bfloat16), ((0, 0), (0, 96)))
+    payload = pl.pallas_call(
+        send_kernel,
+        out_shape=jax.ShapeDtypeStruct((16, ROWS, LANES), jnp.float32),
+        in_specs=[VMEM] * 5,
+        out_specs=VMEM,
+        scratch_shapes=[
+            pltpu.VMEM((4, 384, LANES), jnp.float32),
+            pltpu.VMEM((3, 320, LANES), jnp.float32),
+        ],
+        compiler_params=pltpu.CompilerParams(vmem_limit_bytes=40 * 1024 * 1024),
+        name="sticks",
+    )(coefficients[0], mask, pick, ids.astype(jnp.float32)[None], z_table())
     received = lax.all_to_all(payload, "fft", split_axis=0, concat_axis=0, tiled=True)
+    received = received.reshape(16 * ROWS, LANES)
 
     core = lax.axis_index("band") % 2
     pool_weight = lax.dynamic_index_in_dim(
@@ -279,9 +380,9 @@
         out_specs=(VMEM, VMEM),
         scratch_shapes=[
             pltpu.VMEM((16, LANES, LANES), jnp.float32),
-            pltpu.VMEM((52 * 64, LANES), jnp.float32),
-            pltpu.VMEM((48 * 64, LANES), jnp.float32),
-            pltpu.VMEM((48 * 64, LANES), jnp.float32),
+            pltpu.VMEM((50 * 64, LANES), jnp.float32),
+            pltpu.VMEM((48 * HELD, LANES), jnp.float32),
+            pltpu.VMEM((48 * HELD, LANES), jnp.float32),
             pltpu.VMEM((PLANES * 96, LANES), jnp.float32),
             pltpu.VMEM((16, LANES), jnp.int32),
             pltpu.SMEM((16, LANES), jnp.int32),
@@ -323,19 +424,21 @@
     y_sin = jnp.concatenate(y_parts[2:], 1)
     hz = jnp.arange(ZSPAN, dtype=jnp.float32)
     z_parts = tables(positions[2], hz, 2.0 * math.pi / NZ, jnp.where(hz == 0.0, 1.0, 2.0))
-    z_rows = jnp.concatenate(
-        [jnp.concatenate(z_parts[:2], 1), jnp.concatenate(z_parts[2:], 1)], 0
-    )
-    high, low = table_halves(z_rows)
-    atom_z = jnp.concatenate([high, high, low], 1)
+
+    def atom_table(reach):
+        plain = jnp.concatenate([part[:, :reach] for part in z_parts[:2]], 1)
+        sloped = jnp.concatenate([part[:, :reach] for part in z_parts[2:]], 1)
+        high, low = table_halves(jnp.concatenate([plain, sloped], 0))
+        return jnp.concatenate([high, high, low], 1)
+
     gy = np.tile(2.0 * np.pi / 96 * np.arange(64), 2)
     gz = 2.0 * np.pi / NZ * np.arange(ZSPAN)
     base = (gy[None, :] ** 2 + gz[:, None] ** 2 + screen).astype(np.float32)
     gx2 = (unit * hx) * (unit * hx)
     spread = pl.pallas_call(
         force_kernel,
-        out_shape=jax.ShapeDtypeStruct((16, 8, LANES), jnp.float32),
-        in_specs=[SMEM] + [VMEM] * 9,
+        out_shape=jax.ShapeDtypeStruct((16, 3, LANES), jnp.float32),
+        in_specs=[SMEM] + [VMEM] * 10,
         out_specs=VMEM,
         scratch_shapes=[
             pltpu.VMEM((3, 128, 128), jnp.float32),
@@ -343,11 +446,23 @@
         ],
         compiler_params=pltpu.CompilerParams(vmem_limit_bytes=40 * 1024 * 1024),
         name="force",
-    )(gx2, own, arrived, base, wave_z, atom_z, x_all, y_cos, y_sin, strength[None])
-    total = jnp.sum(lax.all_to_all(spread, ("pool", "band"), 0, 0, tiled=True), axis=0)
-    spread = jnp.broadcast_to(total[None], (16, 8, LANES))
-    total = jnp.sum(lax.all_to_all(spread, "fft", 0, 0, tiled=True), axis=0)
-    return total[:3]
+    )(
+        gx2,
+        own,
+        arrived,
+        base,
+        wave_z,
+        atom_table(ZSPAN),
+        atom_table(NEAR),
+        x_all,
+        y_cos,
+        y_sin,
+        strength[None],
+    )
+    across, along = reduce_groups()
+    total = jnp.sum(lax.all_to_all(spread, AXES, 0, 0, axis_index_groups=across, tiled=True), axis=0)
+    spread = jnp.broadcast_to(total[None], (16, 3, LANES))
+    return jnp.sum(lax.all_to_all(spread, AXES, 0, 0, axis_index_groups=along, tiled=True), axis=0)
 
 
 def solution(mesh):

time: 88.7 us -> 78.7 us (0.89)
  Pallas kernels: 20.7 us -> 16.3 us
  waiting for transfers between devices: 15.1 us -> 13 us
  local copies, waits for them, and re-layouts: 7.3 us -> 5.46 us
  matrix products: 1.26 us -> 0 us
    pallas_call x1, Pallas kernels: 13.7 us -> 8.06 us  [shards(): pl.pallas_call(density_kernel, out_shape=(halves_shape, halves_shape), in...]
    all_to_all x1, waiting for transfers between devices: 14.3 us -> 12.2 us  [shards(): lax.all_to_all(payload, 'fft', split_axis=0, concat_axis=0, tiled=True)]
    another operation x1 -> x0, local copies, waits for them, and re-layouts: 1.48 us -> none  [shards(): shaped = coefficients[0].reshape(4, 2, sticks, ZSPAN)]
    pallas_call x1 -> x2, Pallas kernels: 6.95 us -> 8.25 us  [the longest x1 6.03 us: shards(): pl.pallas_call(force_kernel, out_shape=jax.ShapeDtypeStruct((16, 3, LANES...]
    dot_general x2 -> x0, matrix products: 1.26 us -> none  [the longest x1 0.75 us: shards(): packed = jnp.einsum('bcst,sj->bctj', masked, pick, precision=HIGH)]
  transfers between devices with their start and end apart: 2 -> 2, of which waited for: 2 -> 2; matrix products, arithmetic and copies ran while one was open for 4% -> 5% of each run, Pallas kernels for 0% -> 0%
where the time goes in v2:
time: 78.7 us; the launch traced here: 78.3 us
  blocking collectives  24.5 us (31%)
  Pallas kernels  16.3 us (21%)
  starting transfers between devices  13.2 us (17%)
  waiting for transfers between devices  13 us (17%)
  local copies, waits for them, and re-layouts  5.46 us (7%)
  other arithmetic  4.08 us (5%)
  between operations  1.78 us (2%)
    all_to_all x1, blocking collectives, shards(): lax.all_to_all(spread, AXES, 0, 0, axis_index_groups=across, tiled=True)  12.7 us
    all_to_all x1, waiting for transfers between devices, shards(): lax.all_to_all(payload, 'fft', split_axis=0, concat_axis=0, tiled=True)  12.2 us
    all_to_all x1, blocking collectives, shards(): lax.all_to_all(spread, AXES, 0, 0, axis_index_groups=along, tiled=True)  11.8 us
    all_to_all x1, starting transfers between devices, shards(): lax.all_to_all(payload, 'fft', split_axis=0, concat_axis=0, tiled=True)  10.1 us
    pallas_call x1, Pallas kernels, shards(): pl.pallas_call(density_kernel, out_shape=(halves_shape, halves_shape), in...  8.06 us
    pallas_call x1, Pallas kernels, shards(): pl.pallas_call(force_kernel, out_shape=jax.ShapeDtypeStruct((16, 3, LANES...  6.03 us
    unnamed x28, local copies, waits for them, and re-layouts  3.59 us
    ppermute x1, starting transfers between devices, shards(): arrived = lax.ppermute(other, 'band', swap)  3.06 us
  transfers between devices with their start and end apart: 2, of which 2 were waited for; matrix products, arithmetic and copies ran while one was open for 5% of the time, Pallas kernels for 0%

profile of v2, /device:TPU:1, one launch (start us, length us, event | category | flops | bytes accessed | tf_op | source)
XLA Modules:
  0.0 78.3 jit_solution(1339299330280206571)
XLA Ops:
  0.0 0.8 %reshape.225 = s32[36,4]{1,0:T(8,128)S(1)} reshape(s32[144]{0:T(256)} %param.18) | data formatting | bytes 1152 | tf_op jit(solution)/shard_map/reshape | solution.py:337
  1.3 0.1 select_reduce_fusion
  1.4 0.1 select_reduce_fusion.1
  1.7 1.0 %copy-done = f32[1,4,2,13824]{3,2,1,0:T(2,128)S(1)} copy-done((f32[1,4,2,13824]{3,2,1,0:T(2,128)S(1)}, f32[1,4,2,13824]{3,2,1,0:T(2,128)}, u32[]{:S(2)}) %copy-start) | copy-done | bytes 442392
  2.7 2.2 %sticks.1 = f32[16,88,128]{2,1,0:T(8,128)} custom-call(f32[4,2,13824]{2,1,0:T(2,128)S(1)} %bitcast.22, f32[160,128]{1,0:T(8,128)S(1)} %fusion.6.mask, bf16[128,256]{1,0:T(8,128)(2,1)S(1)} %pad_convert_fusion.pick, f32[1,128]{1,0:T(1,128)S(1)} %convert_bitcast_fusion.ids, bf16[384,256]{1,0:T(8,128)(2,1)S(1)} %copy-done.2), custom_call_target="tpu_custom_call" | custom-call | tf_op jit(solution)/shard_map/sticks/pallas_call | solution.py:353
  4.9 10.1 %all-to-all-start = ((f32[16,88,128]{2,1,0:T(8,128)}), f32[16,88,128]{2,1,0:T(8,128)S(1)}, u32[]{:S(2)}, u32[]{:S(2)}) async-start(f32[16,88,128]{2,1,0:T(8,128)} %sticks.1), calls=%async_computation | async-start | bytes 1441792 | tf_op jit(solution)/shard_map/all_to_all | solution.py:365
  15.2 0.6 copy-done.12
  15.8 0.7 reduce_sum.63
  16.5 0.6 dynamic_slice.8
  18.6 0.7 copy-done.8
  19.3 0.1 fusion.15
  19.5 0.1 copy.33
  19.7 0.3 cosine_multiply_fusion.1
  20.0 0.1 pad_maximum_fusion.2.x_all
  20.2 0.8 copy-done.7
  21.0 0.3 broadcast_multiply_fusion.1
  21.3 0.1 pad_maximum_fusion.3
  21.4 0.3 cosine_multiply_fusion.2
  21.8 0.1 reduce-precision_convert_fusion.1
  22.0 0.4 copy-done.13
  22.4 12.2 %all-to-all-done = f32[16,88,128]{2,1,0:T(8,128)S(1)} async-done(((f32[16,88,128]{2,1,0:T(8,128)}), f32[16,88,128]{2,1,0:T(8,128)S(1)}, u32[]{:S(2)}, u32[]{:S(2)}) %all-to-all-start) | async-done | bytes 720928 | tf_op jit(solution)/shard_map/all_to_all | solution.py:365
  34.6 8.1 %density.1 = (f32[800,128]{1,0:T(8,128)S(1)}, f32[800,128]{1,0:T(8,128)S(1)}) custom-call(f32[4]{0:T(128)S(1)} %multiply_bitcast_fusion.factors, f32[1408,128]{1,0:T(8,128)S(1)} %bitcast.21, bf16[2,256,256]{2,1,0:T(8,128)(2,1)S(1)} %copy-done.1, bf16[192,192]{1,0:T(8,128)(2,1)S(1)} %copy-done.3, bf16[256,128]{1,0:T(8,128)(2,1)S(1)} %copy-done.4, ...), custom_call_target="tpu_custom_call" | custom-call | tf_op jit(solution)/shard_map/density/pallas_call | solution.py:376
  42.7 3.1 %collective-permute-start = (f32[800,128]{1,0:T(8,128)S(1)}, f32[800,128]{1,0:T(8,128)S(1)}, u32[]{:S(2)}, u32[]{:S(2)}) collective-permute-start(f32[800,128]{1,0:T(8,128)S(1)} %get-tuple-element.8), channel_id=1, source_target_pairs={{0,16},{16,0},{32,48},{48,32},{64,80},{80,64},{96,112},{112,96},{1... | collective-permute-start | bytes 1228808 | tf_op jit(solution)/shard_map/ppermute | solution.py:395
  45.7 0.1 pad_maximum_fusion.5.wave_z
  45.8 0.1 reduce-precision_convert_fusion
  46.0 0.2 pad_maximum_fusion.1.near_z
  46.2 0.1 pad_maximum_fusion.atom_z
  46.3 0.8 %collective-permute-done.arrived = f32[800,128]{1,0:T(8,128)S(1)} collective-permute-done((f32[800,128]{1,0:T(8,128)S(1)}, f32[800,128]{1,0:T(8,128)S(1)}, u32[]{:S(2)}, u32[]{:S(2)}) %collective-permute-start) | collective-permute-done | bytes 409632 | tf_op jit(solution)/shard_map/ppermute | solution.py:395
  47.1 6.0 %force.1 = f32[16,3,128]{2,1,0:T(4,128)S(1)} custom-call(f32[32]{0:T(128)S(1)} %fusion.27.gx2, f32[800,128]{1,0:T(8,128)S(1)} %get-tuple-element.7.own, f32[800,128]{1,0:T(8,128)S(1)} %collective-permute-done.arrived, f32[96,128]{1,0:T(8,128)S(1)} %copy-done.5, bf16[192,48]{1,0:T(8,128)(2,1)S(1)} %pad_maximum_fusion.5.wave_z, ...), custom_call_target="tpu_custom_call" | custom-call | tf_op jit(solution)/shard_map/force/pallas_call | solution.py:438
  53.2 12.7 %all_to_all.15 = f32[16,3,128]{2,1,0:T(4,128)S(1)} all-to-all(f32[16,3,128]{2,1,0:T(4,128)S(1)} %force.1), channel_id=1, replica_groups={{0,32,64,96,1,33,65,97,128,160,192,224,129,161,193,225},{16,48,80,112,1..., dimensions={0} | all-to-all | bytes 49152 | tf_op jit(solution)/shard_map/all_to_all | solution.py:463
  65.9 11.8 %all_to_all.16 = f32[16,3,128]{2,1,0:T(4,128)S(1)} all-to-all(f32[16,3,128]{2,1,0:T(4,128)S(1)} %broadcast_in_dim.124), channel_id=1, replica_groups={{0,16,2,18,4,20,6,22,8,24,10,26,12,28,14,30},{32,48,34,50,36,52,38,54,4..., dimensions={0} | all-to-all | bytes 49152 | tf_op jit(solution)/shard_map/all_to_all | solution.py:465
  77.7 0.6 reduce_sum.69
  (56 shorter events, 1.0 us)
Async XLA Ops:
  0.0 1.7 %copy-start.2 = (bf16[384,256]{1,0:T(8,128)(2,1)S(1)}, bf16[384,256]{1,0:T(8,128)(2,1)}, u32[]{:S(2)}) copy-start(bf16[384,256]{1,0:T(8,128)(2,1)} %constant.146.clone.table) | copy-start | bytes 589828
  1.7 1.0 %copy-start = (f32[1,4,2,13824]{3,2,1,0:T(2,128)S(1)}, f32[1,4,2,13824]{3,2,1,0:T(2,128)}, u32[]{:S(2)}) copy-start(f32[1,4,2,13824]{3,2,1,0:T(2,128)} %param.15) | copy-start | bytes 1327108
  4.9 29.7 %all-to-all-start = ((f32[16,88,128]{2,1,0:T(8,128)}), f32[16,88,128]{2,1,0:T(8,128)S(1)}, u32[]{:S(2)}, u32[]{:S(2)}) async-start(f32[16,88,128]{2,1,0:T(8,128)} %sticks.1), calls=%async_computation | async-start | bytes 1441792 | tf_op jit(solution)/shard_map/all_to_all | solution.py:365
  15.2 0.7 copy-start.12
  17.8 0.7 copy-start.9
  17.8 0.7 copy-start.10
  17.8 0.7 copy-start.11
  18.6 0.7 copy-start.8
  20.0 0.9 %copy-start.7 = (bf16[2,128,288]{2,1,0:T(8,128)(2,1)S(1)}, bf16[2,128,288]{2,1,0:T(8,128)(2,1)}, u32[]{:S(2)}) copy-start(bf16[2,128,288]{2,1,0:T(8,128)(2,1)} %constant.147.clone) | copy-start | bytes 442372
  21.8 0.7 copy-start.13
  21.8 12.8 %copy-start.1 = (bf16[2,256,256]{2,1,0:T(8,128)(2,1)S(1)}, bf16[2,256,256]{2,1,0:T(8,128)(2,1)}, u32[]{:S(2)}) copy-start(bf16[2,256,256]{2,1,0:T(8,128)(2,1)} %constant.148.clone.inv_y) | copy-start | bytes 786436
  21.8 12.8 %copy-start.3 = (bf16[192,192]{1,0:T(8,128)(2,1)S(1)}, bf16[192,192]{1,0:T(8,128)(2,1)}, u32[]{:S(2)}) copy-start(bf16[192,192]{1,0:T(8,128)(2,1)} %constant.149.clone.inv_x) | copy-start | bytes 221188
  21.8 12.8 %copy-start.4 = (bf16[256,128]{1,0:T(8,128)(2,1)S(1)}, bf16[256,128]{1,0:T(8,128)(2,1)}, u32[]{:S(2)}) copy-start(bf16[256,128]{1,0:T(8,128)(2,1)} %constant.150.clone.fwd_y1) | copy-start | bytes 196612
  21.8 12.8 %copy-start.6 = (bf16[128,128]{1,0:T(8,128)(2,1)S(1)}, bf16[128,128]{1,0:T(8,128)(2,1)}, u32[]{:S(2)}) copy-start(bf16[128,128]{1,0:T(8,128)(2,1)} %constant.151.clone.fwd_y2) | copy-start | bytes 98308
  42.7 4.4 %collective-permute-start = (f32[800,128]{1,0:T(8,128)S(1)}, f32[800,128]{1,0:T(8,128)S(1)}, u32[]{:S(2)}, u32[]{:S(2)}) collective-permute-start(f32[800,128]{1,0:T(8,128)S(1)} %get-tuple-element.8), channel_id=1, source_target_pairs={{0,16},{16,0},{32,48},{48,32},{64,80},{80,64},{96,112},{112,96},{1... | collective-permute-start | bytes 1228808 | tf_op jit(solution)/shard_map/ppermute | solution.py:395
  46.2 1.0 %copy-start.5 = (f32[96,128]{1,0:T(8,128)S(1)}, f32[96,128]{1,0:T(8,128)}, u32[]{:S(2)}) copy-start(f32[96,128]{1,0:T(8,128)} %constant.152.clone.base) | copy-start | bytes 147460

commit v3 on v2

--- a/solution.py
+++ b/solution.py
@@ -33,13 +33,14 @@
 SMEM = pl.BlockSpec(memory_space=pltpu.SMEM)
 
 
-def signed_freq(offsets, length):
-    return (offsets + length // 2) % length - length // 2
-
-
 def trig(rows, columns, length):
     angles = 2.0 * np.pi / length * (np.outer(rows, columns) % length)
     return np.cos(angles).astype(np.float32), np.sin(angles).astype(np.float32)
+
+
+def exchange_groups():
+    ranks = np.arange(256).reshape(16, 8, 2)
+    return ranks.transpose(0, 2, 1).reshape(16, 16).tolist()
 
 
 def reduce_groups():
@@ -123,6 +124,10 @@
     )
 
 
+def small(flags):
+    return flags.astype(jnp.float32).astype(jnp.bfloat16)
+
+
 def pieces(held, dest, tile):
     found = []
     for row in range(tile * 8, tile * 8 + 8, 4):
@@ -131,35 +136,68 @@
     return jnp.concatenate(found, 0)
 
 
-def send_kernel(coefs, mask, pick, ids, table, out, held, rows):
-    for chunk in range(3 * GROUPS):
-        piece = coefs[:, :, chunk * LANES : (chunk + 1) * LANES]
-        for band in range(4):
-            for part in range(2):
-                start = (band * 2 + part) * 40 + chunk // 3
-                rows[chunk % 3, start : start + 1, :] = piece[band, part : part + 1]
+def send_kernel(cells, coefs, z_waves, out, raw, table, held, natural, rows, loads):
+    copies = [
+        pltpu.make_async_copy(coefs.at[0, band], raw.at[band], loads.at[band]) for band in range(4)
+    ]
+    copies.append(pltpu.make_async_copy(z_waves, table, loads.at[4]))
+    for copy in copies:
+        copy.start()
+    stick = jnp.concatenate([cells[...], jnp.full((1, 112), 48 * NY, jnp.int32)], 1)
+    stick = jnp.broadcast_to(stick, (8, 256))
+    column = stick // NY
+    freq_x = jnp.where(column < 48, column, column - NX)
+    freq_y = stick - column * NY
+    freq_y = jnp.where(freq_y < 48, freq_y, freq_y - NY)
+    reach = freq_x * freq_x + freq_y * freq_y
+    chosen = reach <= HALF * HALF
+    earlier = lax.broadcasted_iota(jnp.int32, (256, 256), 0)
+    earlier = earlier < lax.broadcasted_iota(jnp.int32, (256, 256), 1)
+    rank = mm(chosen.astype(jnp.float32).astype(jnp.bfloat16), small(earlier))
+    order = lax.broadcasted_iota(jnp.int32, (LANES, 256), 0).astype(jnp.float32)
+    pick = small((rank[0:1] == order) & chosen[0:1])
+    line = lax.broadcasted_iota(jnp.int32, (8, 256), 0)
+    facts = jnp.where(line == 0, (freq_x + HALF) * 64, jnp.where(line == 1, freq_y + HALF, 1))
+    facts = mm_t(facts.astype(jnp.float32).astype(jnp.bfloat16), pick)
+    ids = facts[0:1] + facts[1:2] + SPARE_ROW * (1.0 - facts[2:3])
+    coarse = reach // 16 * 16
+    spread = [jnp.broadcast_to(part[0:1], (LANES, 256)) for part in (coarse, reach - coarse)]
+    level = sum(mm_t(pick, part.astype(jnp.float32).astype(jnp.bfloat16)) for part in spread)
+    slot = lax.broadcasted_iota(jnp.int32, (LANES, LANES), 1)
+    freq_z = (slot - NZ // 4).astype(jnp.float32)
+    inside = (16.0 * level + 4.0 * freq_z * freq_z <= NX * NX) & (slot < ZSPAN)
+    inside = jnp.concatenate([inside, inside], 1)
+    for copy in copies:
+        copy.wait()
     high_table = table[:, :LANES]
     wide_table = jnp.concatenate([high_table, high_table], 1)
     low_table = table[:, LANES:]
-    low_lane = lax.broadcasted_iota(jnp.int32, (40, LANES), 1)
-    filler = jnp.zeros((96, 256), jnp.bfloat16)
+    lane = lax.broadcasted_iota(jnp.int32, (40, LANES), 1)
+    filler = jnp.zeros((112, 256), jnp.bfloat16)
     for band in range(4):
         highs, lows = [], []
+        for chunk in range(3 * GROUPS):
+            piece = raw[band, :, chunk * LANES : (chunk + 1) * LANES]
+            for part in range(2):
+                start = part * 40 + chunk // 3
+                rows[band, chunk % 3, start : start + 1, :] = piece[part : part + 1]
         for part in range(2):
-            span = slice((band * 2 + part) * 40, (band * 2 + part) * 40 + 40)
-            first, second, third = rows[0, span, :], rows[1, span, :], rows[2, span, :]
+            span = slice(part * 40, part * 40 + 40)
+            first, second, third = rows[band, 0, span, :], rows[band, 1, span, :], rows[band, 2, span, :]
             quarters = [
                 first,
-                jnp.where(low_lane < 32, pltpu.roll(first, 32, 1), pltpu.roll(second, 32, 1)),
-                jnp.where(low_lane < 64, pltpu.roll(second, 64, 1), pltpu.roll(third, 64, 1)),
+                jnp.where(lane < 32, pltpu.roll(first, 32, 1), pltpu.roll(second, 32, 1)),
+                jnp.where(lane < 64, pltpu.roll(second, 64, 1), pltpu.roll(third, 64, 1)),
                 pltpu.roll(third, 96, 1),
             ]
-            values = jnp.concatenate(quarters, 0)
-            values = jnp.where(mask[...] > 0.0, values, 0.0)
+            for index in range(4):
+                natural[band, pl.ds(part * 144 + index, GROUPS, stride=4), :] = quarters[index][:GROUPS]
+            values = natural[band, part * 144 : part * 144 + 144, :]
             both = jnp.concatenate(halves(values), 1)
-            chosen = mm(pick[...], jnp.concatenate([both, filler], 0))
-            highs.append(chosen[:, :128].astype(jnp.bfloat16))
-            lows.append(chosen[:, 128:].astype(jnp.bfloat16))
+            taken = mm(pick, jnp.concatenate([both, filler], 0))
+            taken = jnp.where(inside, taken, 0.0).astype(jnp.bfloat16)
+            highs.append(taken[:, :128])
+            lows.append(taken[:, 128:])
         high = jnp.concatenate(highs, 0)
         spread = jnp.concatenate([high, jnp.concatenate(lows, 0)], 1)
         waves = mm_t(wide_table, spread) + mm_t(low_table, high)
@@ -169,7 +207,7 @@
     lane = lax.broadcasted_iota(jnp.int32, (8, LANES), 1)
     row = lax.broadcasted_iota(jnp.int32, (8, LANES), 0)
     marks = jnp.zeros((8, LANES), jnp.float32)
-    spots = jnp.broadcast_to(ids[...], (8, LANES))
+    spots = jnp.broadcast_to(ids, (8, LANES))
     for index in range(8):
         marks = jnp.where(row == index, pltpu.roll(spots, STICK_LIMIT - SPARE * index, 1), marks)
     for dest in range(16):
@@ -334,35 +372,23 @@
 def shards(
     coefficients, occupation, kpoint_weight, stick_cell, species, positions, amplitude, core_width
 ):
-    cells = jnp.pad(stick_cell.reshape(GROUPS, 4).T, ((0, 0), (0, 4)), constant_values=48 * NY)
-    cells = cells.reshape(160)
-    freq_x = signed_freq(cells // NY, NX)
-    freq_y = signed_freq(cells % NY, NY)
-    freq_z = jnp.arange(LANES, dtype=jnp.int32) - NZ // 4
-    disk = 16 * (freq_x * freq_x + freq_y * freq_y)
-    level = disk[:, None] + 4 * (freq_z * freq_z)[None, :]
-    mask = ((level <= NX * NX) & (freq_z < NZ // 4)[None, :]).astype(jnp.float32)
-    chosen = disk <= NX * NX
-    before = jnp.arange(160)[:, None] < jnp.arange(160)[None, :]
-    rank = jnp.sum(jnp.where(before & chosen[:, None], 1, 0), axis=0)
-    lane = jnp.arange(LANES, dtype=jnp.int32)
-    pick = chosen[None, :] & (rank[None, :] == lane[:, None])
-    place = (freq_x + HALF) * 64 + freq_y + HALF
-    ids = jnp.sum(jnp.where(pick, place[None, :] - SPARE_ROW, 0), axis=1) + SPARE_ROW
-    pick = jnp.pad(pick.astype(jnp.bfloat16), ((0, 0), (0, 96)))
     payload = pl.pallas_call(
         send_kernel,
         out_shape=jax.ShapeDtypeStruct((16, ROWS, LANES), jnp.float32),
-        in_specs=[VMEM] * 5,
+        in_specs=[VMEM, pl.BlockSpec(memory_space=pltpu.HBM), pl.BlockSpec(memory_space=pltpu.HBM)],
         out_specs=VMEM,
         scratch_shapes=[
+            pltpu.VMEM((4, 2, 13824), jnp.float32),
+            pltpu.VMEM((384, 256), jnp.bfloat16),
             pltpu.VMEM((4, 384, LANES), jnp.float32),
-            pltpu.VMEM((3, 320, LANES), jnp.float32),
+            pltpu.VMEM((4, 288, LANES), jnp.float32),
+            pltpu.VMEM((4, 3, 80, LANES), jnp.float32),
+            pltpu.SemaphoreType.DMA((5,)),
         ],
-        compiler_params=pltpu.CompilerParams(vmem_limit_bytes=40 * 1024 * 1024),
+        compiler_params=pltpu.CompilerParams(vmem_limit_bytes=60 * 1024 * 1024),
         name="sticks",
-    )(coefficients[0], mask, pick, ids.astype(jnp.float32)[None], z_table())
-    received = lax.all_to_all(payload, "fft", split_axis=0, concat_axis=0, tiled=True)
+    )(stick_cell[None], coefficients, z_table())
+    received = lax.all_to_all(payload, AXES, 0, 0, axis_index_groups=exchange_groups(), tiled=True)
     received = received.reshape(16 * ROWS, LANES)
 
     core = lax.axis_index("band") % 2
@@ -394,7 +420,8 @@
     swap = [(index, index ^ 1) for index in range(8)]
     arrived = lax.ppermute(other, "band", swap)
 
-    start = lax.axis_index("fft") * PLANES
+    rank_z, rank_y = lax.axis_index("fft") // 2, lax.axis_index("fft") % 2
+    start = (rank_y * 8 + rank_z) * PLANES
     steps = (jnp.arange(ZSPAN)[:, None] * (start + jnp.arange(PLANES))[None, :]) % NZ
     angles = 2.0 * math.pi / NZ * steps.astype(jnp.float32)
     turned = jnp.pad(jnp.concatenate([jnp.cos(angles), jnp.sin(angles)], 0), ((0, 0), (0, 4)))

time: 78.7 us -> 77.1 us (0.980)
  local copies, waits for them, and re-layouts: 5.46 us -> 3.37 us
  Pallas kernels: 16.3 us -> 18.3 us
  waiting for transfers between devices: 13 us -> 11.9 us
  blocking collectives: 24.5 us -> 25.4 us
    pallas_call x1, Pallas kernels: 2.22 us -> 4.13 us  [shards(): pl.pallas_call(send_kernel, out_shape=jax.ShapeDtypeStruct((16, ROWS, LAN...]
    all_to_all x1, waiting for transfers between devices: 12.2 us -> 11.1 us  [shards(): lax.all_to_all(payload, AXES, 0, 0, axis_index_groups=exchange_groups(),...]
    unnamed x28 -> x24, local copies, waits for them, and re-layouts: 3.59 us -> 2.65 us
    reshape x2 -> x0, local copies, waits for them, and re-layouts: 0.9 us -> none  [shards(): stick_cell.reshape(GROUPS, 4)]
    all_to_all x1, blocking collectives: 11.8 us -> 12.7 us  [shards(): lax.all_to_all(spread, AXES, 0, 0, axis_index_groups=along, tiled=True)]
where the time goes in v3:
time: 77.1 us; the launch traced here: 76.7 us
  blocking collectives  25.4 us (33%)
  Pallas kernels  18.3 us (24%)
  starting transfers between devices  12.7 us (16%)
  waiting for transfers between devices  11.9 us (15%)
  other arithmetic  3.53 us (5%)
  local copies, waits for them, and re-layouts  3.37 us (4%)
  between operations  1.57 us (2%)
    all_to_all x1, blocking collectives, shards(): lax.all_to_all(spread, AXES, 0, 0, axis_index_groups=across, tiled=True)  12.7 us
    all_to_all x1, blocking collectives, shards(): lax.all_to_all(spread, AXES, 0, 0, axis_index_groups=along, tiled=True)  12.7 us
    all_to_all x1, waiting for transfers between devices, shards(): lax.all_to_all(payload, AXES, 0, 0, axis_index_groups=exchange_groups(),...  11.1 us
    all_to_all x1, starting transfers between devices, shards(): lax.all_to_all(payload, AXES, 0, 0, axis_index_groups=exchange_groups(),...  10.1 us
    pallas_call x1, Pallas kernels, shards(): pl.pallas_call(density_kernel, out_shape=(halves_shape, halves_shape), in...  8.16 us
    pallas_call x1, Pallas kernels, shards(): pl.pallas_call(force_kernel, out_shape=jax.ShapeDtypeStruct((16, 3, LANES...  6.03 us
    pallas_call x1, Pallas kernels, shards(): pl.pallas_call(send_kernel, out_shape=jax.ShapeDtypeStruct((16, ROWS, LAN...  4.13 us
    unnamed x24, local copies, waits for them, and re-layouts  2.65 us
  transfers between devices with their start and end apart: 2, of which 2 were waited for; matrix products, arithmetic and copies ran while one was open for 5% of the time, Pallas kernels for 0%

profile of v3, /device:TPU:1, one launch (start us, length us, event | category | flops | bytes accessed | tf_op | source)
XLA Modules:
  0.0 76.7 jit_solution(14025019469812577016)
XLA Ops:
  0.0 4.1 %sticks.1 = f32[16,88,128]{2,1,0:T(8,128)} custom-call(s32[1,144]{1,0:T(1,128)} %bitcast.24, f32[1,4,2,13824]{3,2,1,0:T(2,128)} %coefs.1, bf16[384,256]{1,0:T(8,128)(2,1)} %constant.108.clone.z_waves), custom_call_target="tpu_custom_call" | custom-call | tf_op jit(solution)/shard_map/sticks/pallas_call | solution.py:375
  4.1 10.1 %all-to-all-start = ((f32[16,88,128]{2,1,0:T(8,128)}), f32[16,88,128]{2,1,0:T(8,128)S(1)}, u32[]{:S(2)}, u32[]{:S(2)}) async-start(f32[16,88,128]{2,1,0:T(8,128)} %sticks.1), calls=%async_computation | async-start | bytes 1441792 | tf_op jit(solution)/shard_map/all_to_all | solution.py:391
  14.4 0.6 copy-done.10
  15.1 0.6 reduce_sum.45
  15.7 0.6 dynamic_slice.8
  17.5 0.1 copy-done.7
  17.6 0.0 copy-done.8
  17.6 0.1 select_reduce_fusion
  17.7 0.7 copy-done.6
  18.4 0.1 fusion.11
  18.5 0.1 pad_maximum_fusion.6
  18.6 0.1 copy.20
  18.8 0.3 cosine_multiply_fusion.1
  19.1 0.1 pad_maximum_fusion.2.x_all
  19.3 0.8 copy-done.5
  20.1 0.3 broadcast_multiply_fusion.1
  20.4 0.1 pad_maximum_fusion.3
  20.5 0.3 cosine_multiply_fusion.2
  20.9 0.1 reduce-precision_convert_fusion.1
  21.0 0.4 copy-done.11
  21.5 11.1 %all-to-all-done = f32[16,88,128]{2,1,0:T(8,128)S(1)} async-done(((f32[16,88,128]{2,1,0:T(8,128)}), f32[16,88,128]{2,1,0:T(8,128)S(1)}, u32[]{:S(2)}, u32[]{:S(2)}) %all-to-all-start) | async-done | bytes 720928 | tf_op jit(solution)/shard_map/all_to_all | solution.py:391
  32.6 8.2 %density.1 = (f32[800,128]{1,0:T(8,128)S(1)}, f32[800,128]{1,0:T(8,128)S(1)}) custom-call(f32[4]{0:T(128)S(1)} %multiply_bitcast_fusion.factors, f32[1408,128]{1,0:T(8,128)S(1)} %bitcast.18, bf16[2,256,256]{2,1,0:T(8,128)(2,1)S(1)} %copy-done, bf16[192,192]{1,0:T(8,128)(2,1)S(1)} %copy-done.1, bf16[256,128]{1,0:T(8,128)(2,1)S(1)} %copy-done.2, ...), custom_call_target="tpu_custom_call" | custom-call | tf_op jit(solution)/shard_map/density/pallas_call | solution.py:402
  40.8 2.5 %collective-permute-start = (f32[800,128]{1,0:T(8,128)S(1)}, f32[800,128]{1,0:T(8,128)S(1)}, u32[]{:S(2)}, u32[]{:S(2)}) collective-permute-start(f32[800,128]{1,0:T(8,128)S(1)} %get-tuple-element.8), channel_id=1, source_target_pairs={{0,16},{16,0},{32,48},{48,32},{64,80},{80,64},{96,112},{112,96},{1... | collective-permute-start | bytes 1228808 | tf_op jit(solution)/shard_map/ppermute | solution.py:421
  43.3 0.1 pad_maximum_fusion.5.wave_z
  43.4 0.1 reduce-precision_convert_fusion
  43.6 0.2 pad_maximum_fusion.1.near_z
  43.7 0.1 pad_maximum_fusion.atom_z
  43.9 0.8 %collective-permute-done.arrived = f32[800,128]{1,0:T(8,128)S(1)} collective-permute-done((f32[800,128]{1,0:T(8,128)S(1)}, f32[800,128]{1,0:T(8,128)S(1)}, u32[]{:S(2)}, u32[]{:S(2)}) %collective-permute-start) | collective-permute-done | bytes 409632 | tf_op jit(solution)/shard_map/ppermute | solution.py:421
  44.7 6.0 %force.1 = f32[16,3,128]{2,1,0:T(4,128)S(1)} custom-call(f32[32]{0:T(128)S(1)} %fusion.18.gx2, f32[800,128]{1,0:T(8,128)S(1)} %get-tuple-element.7.own, f32[800,128]{1,0:T(8,128)S(1)} %collective-permute-done.arrived, f32[96,128]{1,0:T(8,128)S(1)} %copy-done.3, bf16[192,48]{1,0:T(8,128)(2,1)S(1)} %pad_maximum_fusion.5.wave_z, ...), custom_call_target="tpu_custom_call" | custom-call | tf_op jit(solution)/shard_map/force/pallas_call | solution.py:465
  50.7 12.7 %all_to_all.15 = f32[16,3,128]{2,1,0:T(4,128)S(1)} all-to-all(f32[16,3,128]{2,1,0:T(4,128)S(1)} %force.1), channel_id=1, replica_groups={{0,32,64,96,1,33,65,97,128,160,192,224,129,161,193,225},{16,48,80,112,1..., dimensions={0} | all-to-all | bytes 49152 | tf_op jit(solution)/shard_map/all_to_all | solution.py:490
  63.5 12.7 %all_to_all.16 = f32[16,3,128]{2,1,0:T(4,128)S(1)} all-to-all(f32[16,3,128]{2,1,0:T(4,128)S(1)} %broadcast_in_dim.93), channel_id=1, replica_groups={{0,16,2,18,4,20,6,22,8,24,10,26,12,28,14,30},{32,48,34,50,36,52,38,54,4..., dimensions={0} | all-to-all | bytes 49152 | tf_op jit(solution)/shard_map/all_to_all | solution.py:492
  76.1 0.6 reduce_sum.49
  (35 shorter events, 0.2 us)
Async XLA Ops:
  4.1 28.5 %all-to-all-start = ((f32[16,88,128]{2,1,0:T(8,128)}), f32[16,88,128]{2,1,0:T(8,128)S(1)}, u32[]{:S(2)}, u32[]{:S(2)}) async-start(f32[16,88,128]{2,1,0:T(8,128)} %sticks.1), calls=%async_computation | async-start | bytes 1441792 | tf_op jit(solution)/shard_map/all_to_all | solution.py:391
  14.4 0.7 copy-start.10
  16.9 0.7 copy-start.7
  16.9 0.7 copy-start.8
  16.9 0.7 copy-start.9
  17.7 0.7 copy-start.6
  19.1 0.9 %copy-start.5 = (bf16[2,128,288]{2,1,0:T(8,128)(2,1)S(1)}, bf16[2,128,288]{2,1,0:T(8,128)(2,1)}, u32[]{:S(2)}) copy-start(bf16[2,128,288]{2,1,0:T(8,128)(2,1)} %constant.109.clone) | copy-start | bytes 442372
  20.8 0.7 copy-start.11
  20.8 11.7 %copy-start = (bf16[2,256,256]{2,1,0:T(8,128)(2,1)S(1)}, bf16[2,256,256]{2,1,0:T(8,128)(2,1)}, u32[]{:S(2)}) copy-start(bf16[2,256,256]{2,1,0:T(8,128)(2,1)} %constant.110.clone.inv_y) | copy-start | bytes 786436
  20.9 11.7 %copy-start.1 = (bf16[192,192]{1,0:T(8,128)(2,1)S(1)}, bf16[192,192]{1,0:T(8,128)(2,1)}, u32[]{:S(2)}) copy-start(bf16[192,192]{1,0:T(8,128)(2,1)} %constant.111.clone.inv_x) | copy-start | bytes 221188
  20.9 11.7 %copy-start.2 = (bf16[256,128]{1,0:T(8,128)(2,1)S(1)}, bf16[256,128]{1,0:T(8,128)(2,1)}, u32[]{:S(2)}) copy-start(bf16[256,128]{1,0:T(8,128)(2,1)} %constant.112.clone.fwd_y1) | copy-start | bytes 196612
  20.9 11.7 %copy-start.4 = (bf16[128,128]{1,0:T(8,128)(2,1)S(1)}, bf16[128,128]{1,0:T(8,128)(2,1)}, u32[]{:S(2)}) copy-start(bf16[128,128]{1,0:T(8,128)(2,1)} %constant.113.clone.fwd_y2) | copy-start | bytes 98308
  40.8 3.9 %collective-permute-start = (f32[800,128]{1,0:T(8,128)S(1)}, f32[800,128]{1,0:T(8,128)S(1)}, u32[]{:S(2)}, u32[]{:S(2)}) collective-permute-start(f32[800,128]{1,0:T(8,128)S(1)} %get-tuple-element.8), channel_id=1, source_target_pairs={{0,16},{16,0},{32,48},{48,32},{64,80},{80,64},{96,112},{112,96},{1... | collective-permute-start | bytes 1228808 | tf_op jit(solution)/shard_map/ppermute | solution.py:421
  43.7 1.0 %copy-start.3 = (f32[96,128]{1,0:T(8,128)S(1)}, f32[96,128]{1,0:T(8,128)}, u32[]{:S(2)}) copy-start(f32[96,128]{1,0:T(8,128)} %constant.114.clone.base) | copy-start | bytes 147460

commit v4 on v3

--- a/solution.py
+++ b/solution.py
@@ -24,12 +24,14 @@
 ROWS = 88
 NEAR = 80
 HELD = 72
+FOLD = 56
 GROUPS = 36
 SPARE_ROW = SIDE * 64
 HIGH = lax.Precision.HIGH
 screen = 0.25
 AXES = ("pool", "band", "fft")
 VMEM = pl.BlockSpec(memory_space=pltpu.VMEM)
+HBM = pl.BlockSpec(memory_space=pltpu.HBM)
 SMEM = pl.BlockSpec(memory_space=pltpu.SMEM)
 
 
@@ -89,9 +91,9 @@
 
 
 def inverse_x_table():
-    cosine, sine = trig(np.arange(96), np.arange(SIDE) - HALF, 96)
-    both = np.zeros((192, 64), np.float32)
-    both[:96, :SIDE], both[96:, :SIDE] = cosine, sine
+    cosine, sine = trig(np.arange(SIDE), np.arange(SIDE) - HALF, 96)
+    both = np.zeros((2 * FOLD, 64), np.float32)
+    both[:SIDE, :SIDE], both[FOLD : FOLD + SIDE, :SIDE] = cosine, sine
     high, low = np_halves(both)
     return np.concatenate([high, high, low], 1)
 
@@ -105,14 +107,15 @@
 
 
 def forward_x_tables():
-    cosine, sine = trig(np.arange(50), np.arange(96), 96)
+    cosine, sine = trig(np.arange(50), np.arange(SIDE), 96)
     cosine[SIDE:], sine[SIDE:] = 0.0, 0.0
+    cosine[:, 0], cosine[:, 48] = cosine[:, 0] / 2, cosine[:, 48] / 2
     result = []
     for core in range(2):
-        both = np.zeros((128, 96), np.float32)
+        both = np.zeros((128, 2 * FOLD), np.float32)
         for index, rows in enumerate((core, 1 - core)):
-            both[64 * index : 64 * index + SLOTS] = cosine[rows::2]
-            both[64 * index + 32 : 64 * index + 32 + SLOTS] = sine[rows::2]
+            both[64 * index : 64 * index + SLOTS, :SIDE] = cosine[rows::2]
+            both[64 * index + 32 : 64 * index + 32 + SLOTS, FOLD : FOLD + SIDE] = sine[rows::2]
         high, low = np_halves(both)
         result.append(np.concatenate([high, high, low], 1))
     return np.stack(result)
@@ -136,14 +139,21 @@
     return jnp.concatenate(found, 0)
 
 
-def send_kernel(cells, coefs, z_waves, out, raw, table, held, natural, rows, loads):
+def send_kernel(
+    cells, coefs, z_waves, out, place, raw, table, held, natural, rows, packed, loads, stores
+):
     copies = [
         pltpu.make_async_copy(coefs.at[0, band], raw.at[band], loads.at[band]) for band in range(4)
     ]
     copies.append(pltpu.make_async_copy(z_waves, table, loads.at[4]))
+    where = pltpu.make_async_copy(cells, place, loads.at[5])
+    where.start()
     for copy in copies:
         copy.start()
-    stick = jnp.concatenate([cells[...], jnp.full((1, 112), 48 * NY, jnp.int32)], 1)
+    where.wait()
+    for copy in copies:
+        copy.wait()
+    stick = jnp.concatenate([place[...], jnp.full((1, 112), 48 * NY, jnp.int32)], 1)
     stick = jnp.broadcast_to(stick, (8, 256))
     column = stick // NY
     freq_x = jnp.where(column < 48, column, column - NX)
@@ -167,8 +177,6 @@
     freq_z = (slot - NZ // 4).astype(jnp.float32)
     inside = (16.0 * level + 4.0 * freq_z * freq_z <= NX * NX) & (slot < ZSPAN)
     inside = jnp.concatenate([inside, inside], 1)
-    for copy in copies:
-        copy.wait()
     high_table = table[:, :LANES]
     wide_table = jnp.concatenate([high_table, high_table], 1)
     low_table = table[:, LANES:]
@@ -210,6 +218,7 @@
     spots = jnp.broadcast_to(ids, (8, LANES))
     for index in range(8):
         marks = jnp.where(row == index, pltpu.roll(spots, STICK_LIMIT - SPARE * index, 1), marks)
+    sent = []
     for dest in range(16):
         tail = pieces(held, dest, 11)
         for tile in range(11):
@@ -218,7 +227,12 @@
                 extra = pltpu.roll(tail, STICK_LIMIT - SPARE * tile, 1)
             else:
                 extra = marks
-            out[dest, tile * 8 : tile * 8 + 8, :] = jnp.where(lane < STICK_LIMIT, main, extra)
+            packed[dest, tile * 8 : tile * 8 + 8, :] = jnp.where(lane < STICK_LIMIT, main, extra)
+        copy = pltpu.make_async_copy(packed.at[dest], out.at[dest], stores.at[dest])
+        copy.start()
+        sent.append(copy)
+    for copy in sent:
+        copy.wait()
 
 
 def density_kernel(
@@ -269,7 +283,7 @@
             grid[pl.ds(ids[source, stick], 1), :] = columns[source, stick : stick + 1, :]
         return 0
 
-    lax.fori_loop(0, 16, put, 0)
+    lax.fori_loop(0, 16, put, 0, unroll=16)
     lower = lax.broadcasted_iota(jnp.int32, (96, 128), 1) < 64
 
     def place(pair, _):
@@ -292,27 +306,32 @@
         other[pl.ds(row, 2 * SLOTS, stride=16), :] = clear
 
     def waves(plane, _):
-        total = jnp.zeros((96, 128), jnp.float32)
+        even = jnp.zeros((FOLD, 128), jnp.float32)
+        odd = jnp.zeros((FOLD, 128), jnp.float32)
         for band in range(4):
             start = pl.multiple_of((band * PLANES + plane) * HELD, HELD)
             rows = pl.ds(start, 64)
             high, low = halves(jnp.concatenate([held_re[rows, :], held_im[rows, :]], 1))
             out = mm(inv_x[...], jnp.concatenate([high, low, high], 0))
-            wave_re = out[:96, :128] - out[96:, 128:]
-            wave_im = out[96:, :128] + out[:96, 128:]
-            total = total + factors[band] * (wave_re * wave_re + wave_im * wave_im)
-        density[pl.ds(pl.multiple_of(plane * 96, 96), 96), :] = total
+            cos_re, cos_im = out[:FOLD, :128], out[:FOLD, 128:]
+            sin_re, sin_im = out[FOLD:, :128], out[FOLD:, 128:]
+            sums = cos_re * cos_re + cos_im * cos_im + (sin_re * sin_re + sin_im * sin_im)
+            even = even + (2.0 * factors[band]) * sums
+            odd = odd + (4.0 * factors[band]) * (cos_im * sin_re - cos_re * sin_im)
+        start = pl.multiple_of(plane * 2 * FOLD, 2 * FOLD)
+        density[pl.ds(start, 2 * FOLD), :] = jnp.concatenate([even, odd], 0)
         return 0
 
-    lax.fori_loop(0, PLANES, waves, 0, unroll=4)
+    lax.fori_loop(0, PLANES, waves, 0, unroll=12)
 
     def forward(group, _):
-        start = pl.multiple_of(group * 384, 384)
-        high, low = halves(density[pl.ds(start, 384), :])
+        start = pl.multiple_of(group * 8 * FOLD, 8 * FOLD)
+        high, low = halves(density[pl.ds(start, 8 * FOLD), :])
         rows = mm(jnp.concatenate([high, low], 1), fwd_y1[...]) + mm(high, fwd_y2[...])
         high, low = halves(rows)
         for pair in range(2):
-            first, second = slice(pair * 192, pair * 192 + 96), slice(pair * 192 + 96, pair * 192 + 192)
+            middle = (4 * pair + 2) * FOLD
+            first, second = slice(middle - 2 * FOLD, middle), slice(middle, middle + 2 * FOLD)
             wide_high = jnp.concatenate([high[first], high[second]], 1)
             wide_low = jnp.concatenate([low[first], low[second]], 1)
             out = mm(fwd_x[...], jnp.concatenate([wide_high, wide_low, wide_high], 0))
@@ -360,7 +379,7 @@
         turn[...] = pltpu.roll(table, 127, 1)
         return 0
 
-    lax.fori_loop(0, 14, lambda slot, _: step(slot, ZSPAN, atom_z), 0, unroll=7)
+    lax.fori_loop(0, 14, lambda slot, _: step(slot, ZSPAN, atom_z), 0, unroll=14)
     lax.fori_loop(14, SLOTS, lambda slot, _: step(slot, NEAR, near_z), 0, unroll=11)
     parts = [acc[0] * y_cos[...], acc[1] * y_sin[...], acc[2] * y_cos[...]]
     rows = [-strength[...] * jnp.sum(part.T, axis=0, keepdims=True) for part in parts]
@@ -375,15 +394,18 @@
     payload = pl.pallas_call(
         send_kernel,
         out_shape=jax.ShapeDtypeStruct((16, ROWS, LANES), jnp.float32),
-        in_specs=[VMEM, pl.BlockSpec(memory_space=pltpu.HBM), pl.BlockSpec(memory_space=pltpu.HBM)],
-        out_specs=VMEM,
+        in_specs=[HBM] * 3,
+        out_specs=HBM,
         scratch_shapes=[
+            pltpu.VMEM((1, 144), jnp.int32),
             pltpu.VMEM((4, 2, 13824), jnp.float32),
             pltpu.VMEM((384, 256), jnp.bfloat16),
             pltpu.VMEM((4, 384, LANES), jnp.float32),
             pltpu.VMEM((4, 288, LANES), jnp.float32),
             pltpu.VMEM((4, 3, 80, LANES), jnp.float32),
-            pltpu.SemaphoreType.DMA((5,)),
+            pltpu.VMEM((16, ROWS, LANES), jnp.float32),
+            pltpu.SemaphoreType.DMA((6,)),
+            pltpu.SemaphoreType.DMA((16,)),
         ],
         compiler_params=pltpu.CompilerParams(vmem_limit_bytes=60 * 1024 * 1024),
         name="sticks",
@@ -409,7 +431,7 @@
             pltpu.VMEM((50 * 64, LANES), jnp.float32),
             pltpu.VMEM((48 * HELD, LANES), jnp.float32),
             pltpu.VMEM((48 * HELD, LANES), jnp.float32),
-            pltpu.VMEM((PLANES * 96, LANES), jnp.float32),
+            pltpu.VMEM((PLANES * 2 * FOLD, LANES), jnp.float32),
             pltpu.VMEM((16, LANES), jnp.int32),
             pltpu.SMEM((16, LANES), jnp.int32),
             pltpu.SemaphoreType.DMA,

time: 77.1 us -> 74.7 us (0.969)
  Pallas kernels: 18.3 us -> 15.8 us
    pallas_call x1, Pallas kernels: 8.16 us -> 6.82 us  [shards(): pl.pallas_call(density_kernel, out_shape=(halves_shape, halves_shape), in...]
where the time goes in v4:
time: 74.7 us; the launch traced here: 74.4 us
  blocking collectives  25.4 us (34%)
  Pallas kernels  15.8 us (21%)
  starting transfers between devices  12.8 us (17%)
  waiting for transfers between devices  11.9 us (16%)
  other arithmetic  3.53 us (5%)
  local copies, waits for them, and re-layouts  3.37 us (5%)
  between operations  1.57 us (2%)
    all_to_all x1, blocking collectives, shards(): lax.all_to_all(spread, AXES, 0, 0, axis_index_groups=across, tiled=True)  12.7 us
    all_to_all x1, blocking collectives, shards(): lax.all_to_all(spread, AXES, 0, 0, axis_index_groups=along, tiled=True)  12.7 us
    all_to_all x1, waiting for transfers between devices, shards(): lax.all_to_all(payload, AXES, 0, 0, axis_index_groups=exchange_groups(),...  11.1 us
    all_to_all x1, starting transfers between devices, shards(): lax.all_to_all(payload, AXES, 0, 0, axis_index_groups=exchange_groups(),...  10.1 us
    pallas_call x1, Pallas kernels, shards(): pl.pallas_call(density_kernel, out_shape=(halves_shape, halves_shape), in...  6.82 us
    pallas_call x1, Pallas kernels, shards(): pl.pallas_call(force_kernel, out_shape=jax.ShapeDtypeStruct((16, 3, LANES...  5.48 us
    pallas_call x1, Pallas kernels, shards(): pl.pallas_call(send_kernel, out_shape=jax.ShapeDtypeStruct((16, ROWS, LAN...  3.47 us
    ppermute x1, starting transfers between devices, shards(): arrived = lax.ppermute(other, 'band', swap)  2.71 us
  transfers between devices with their start and end apart: 2, of which 2 were waited for; matrix products, arithmetic and copies ran while one was open for 5% of the time, Pallas kernels for 0%

profile of v4, /device:TPU:1, one launch (start us, length us, event | category | flops | bytes accessed | tf_op | source)
XLA Modules:
  0.0 74.4 jit_solution(3522161928697292568)
XLA Ops:
  0.0 3.5 %sticks.1 = f32[16,88,128]{2,1,0:T(8,128)} custom-call(s32[1,144]{1,0:T(1,128)} %bitcast.24, f32[1,4,2,13824]{3,2,1,0:T(2,128)} %coefs.1, bf16[384,256]{1,0:T(8,128)(2,1)} %constant.108.clone.z_waves), custom_call_target="tpu_custom_call" | custom-call | tf_op jit(solution)/shard_map/sticks/pallas_call | solution.py:394
  3.5 10.1 %all-to-all-start = ((f32[16,88,128]{2,1,0:T(8,128)}), f32[16,88,128]{2,1,0:T(8,128)S(1)}, u32[]{:S(2)}, u32[]{:S(2)}) async-start(f32[16,88,128]{2,1,0:T(8,128)} %sticks.1), calls=%async_computation | async-start | bytes 1441792 | tf_op jit(solution)/shard_map/all_to_all | solution.py:413
  13.8 0.6 copy-done.10
  14.4 0.6 reduce_sum.45
  15.0 0.6 dynamic_slice.8
  16.9 0.1 copy-done.7
  16.9 0.0 copy-done.8
  16.9 0.1 select_reduce_fusion
  17.1 0.7 copy-done.6
  17.7 0.1 fusion.11
  17.9 0.1 pad_maximum_fusion.6
  17.9 0.1 copy.20
  18.1 0.3 cosine_multiply_fusion.1
  18.5 0.1 pad_maximum_fusion.2.x_all
  18.6 0.8 %copy-done.5 = bf16[2,128,336]{2,1,0:T(8,128)(2,1)S(1)} copy-done((bf16[2,128,336]{2,1,0:T(8,128)(2,1)S(1)}, bf16[2,128,336]{2,1,0:T(8,128)(2,1)}, u32[]{:S(2)}) %copy-start.5) | copy-done | bytes 172056
  19.4 0.3 broadcast_multiply_fusion.1
  19.7 0.1 pad_maximum_fusion.3
  19.8 0.3 cosine_multiply_fusion.2
  20.2 0.1 reduce-precision_convert_fusion.1
  20.4 0.4 copy-done.11
  20.8 11.1 %all-to-all-done = f32[16,88,128]{2,1,0:T(8,128)S(1)} async-done(((f32[16,88,128]{2,1,0:T(8,128)}), f32[16,88,128]{2,1,0:T(8,128)S(1)}, u32[]{:S(2)}, u32[]{:S(2)}) %all-to-all-start) | async-done | bytes 720928 | tf_op jit(solution)/shard_map/all_to_all | solution.py:413
  32.0 6.8 %density.1 = (f32[800,128]{1,0:T(8,128)S(1)}, f32[800,128]{1,0:T(8,128)S(1)}) custom-call(f32[4]{0:T(128)S(1)} %multiply_bitcast_fusion.factors, f32[1408,128]{1,0:T(8,128)S(1)} %bitcast.18, bf16[2,256,256]{2,1,0:T(8,128)(2,1)S(1)} %copy-done, bf16[112,192]{1,0:T(8,128)(2,1)S(1)} %copy-done.2, bf16[256,128]{1,0:T(8,128)(2,1)S(1)} %copy-done.1, ...), custom_call_target="tpu_custom_call" | custom-call | tf_op jit(solution)/shard_map/density/pallas_call | solution.py:424
  38.8 2.7 %collective-permute-start = (f32[800,128]{1,0:T(8,128)S(1)}, f32[800,128]{1,0:T(8,128)S(1)}, u32[]{:S(2)}, u32[]{:S(2)}) collective-permute-start(f32[800,128]{1,0:T(8,128)S(1)} %get-tuple-element.8), channel_id=1, source_target_pairs={{0,16},{16,0},{32,48},{48,32},{64,80},{80,64},{96,112},{112,96},{1... | collective-permute-start | bytes 1228808 | tf_op jit(solution)/shard_map/ppermute | solution.py:443
  41.5 0.1 pad_maximum_fusion.5.wave_z
  41.6 0.1 reduce-precision_convert_fusion
  41.7 0.2 pad_maximum_fusion.1.near_z
  41.9 0.1 pad_maximum_fusion.atom_z
  42.0 0.8 %collective-permute-done.arrived = f32[800,128]{1,0:T(8,128)S(1)} collective-permute-done((f32[800,128]{1,0:T(8,128)S(1)}, f32[800,128]{1,0:T(8,128)S(1)}, u32[]{:S(2)}, u32[]{:S(2)}) %collective-permute-start) | collective-permute-done | bytes 409632 | tf_op jit(solution)/shard_map/ppermute | solution.py:443
  42.9 5.5 %force.1 = f32[16,3,128]{2,1,0:T(4,128)S(1)} custom-call(f32[32]{0:T(128)S(1)} %fusion.18.gx2, f32[800,128]{1,0:T(8,128)S(1)} %get-tuple-element.7.own, f32[800,128]{1,0:T(8,128)S(1)} %collective-permute-done.arrived, f32[96,128]{1,0:T(8,128)S(1)} %copy-done.3, bf16[192,48]{1,0:T(8,128)(2,1)S(1)} %pad_maximum_fusion.5.wave_z, ...), custom_call_target="tpu_custom_call" | custom-call | tf_op jit(solution)/shard_map/force/pallas_call | solution.py:487
  48.3 12.7 %all_to_all.15 = f32[16,3,128]{2,1,0:T(4,128)S(1)} all-to-all(f32[16,3,128]{2,1,0:T(4,128)S(1)} %force.1), channel_id=1, replica_groups={{0,32,64,96,1,33,65,97,128,160,192,224,129,161,193,225},{16,48,80,112,1..., dimensions={0} | all-to-all | bytes 49152 | tf_op jit(solution)/shard_map/all_to_all | solution.py:512
  61.1 12.7 %all_to_all.16 = f32[16,3,128]{2,1,0:T(4,128)S(1)} all-to-all(f32[16,3,128]{2,1,0:T(4,128)S(1)} %broadcast_in_dim.93), channel_id=1, replica_groups={{0,16,2,18,4,20,6,22,8,24,10,26,12,28,14,30},{32,48,34,50,36,52,38,54,4..., dimensions={0} | all-to-all | bytes 49152 | tf_op jit(solution)/shard_map/all_to_all | solution.py:514
  73.8 0.6 reduce_sum.49
  (35 shorter events, 0.2 us)
Async XLA Ops:
  3.5 28.4 %all-to-all-start = ((f32[16,88,128]{2,1,0:T(8,128)}), f32[16,88,128]{2,1,0:T(8,128)S(1)}, u32[]{:S(2)}, u32[]{:S(2)}) async-start(f32[16,88,128]{2,1,0:T(8,128)} %sticks.1), calls=%async_computation | async-start | bytes 1441792 | tf_op jit(solution)/shard_map/all_to_all | solution.py:413
  13.8 0.7 copy-start.10
  16.3 0.7 copy-start.7
  16.3 0.7 copy-start.8
  16.3 0.7 copy-start.9
  17.0 0.7 copy-start.6
  18.4 0.9 %copy-start.5 = (bf16[2,128,336]{2,1,0:T(8,128)(2,1)S(1)}, bf16[2,128,336]{2,1,0:T(8,128)(2,1)}, u32[]{:S(2)}) copy-start(bf16[2,128,336]{2,1,0:T(8,128)(2,1)} %constant.109.clone) | copy-start | bytes 516100
  20.2 0.7 copy-start.11
  20.2 11.7 %copy-start = (bf16[2,256,256]{2,1,0:T(8,128)(2,1)S(1)}, bf16[2,256,256]{2,1,0:T(8,128)(2,1)}, u32[]{:S(2)}) copy-start(bf16[2,256,256]{2,1,0:T(8,128)(2,1)} %constant.110.clone.inv_y) | copy-start | bytes 786436
  20.2 11.7 %copy-start.1 = (bf16[256,128]{1,0:T(8,128)(2,1)S(1)}, bf16[256,128]{1,0:T(8,128)(2,1)}, u32[]{:S(2)}) copy-start(bf16[256,128]{1,0:T(8,128)(2,1)} %constant.112.clone.fwd_y1) | copy-start | bytes 196612
  20.2 11.7 %copy-start.2 = (bf16[112,192]{1,0:T(8,128)(2,1)S(1)}, bf16[112,192]{1,0:T(8,128)(2,1)}, u32[]{:S(2)}) copy-start(bf16[112,192]{1,0:T(8,128)(2,1)} %constant.111.clone.inv_x) | copy-start | bytes 129028
  20.2 11.7 %copy-start.4 = (bf16[128,128]{1,0:T(8,128)(2,1)S(1)}, bf16[128,128]{1,0:T(8,128)(2,1)}, u32[]{:S(2)}) copy-start(bf16[128,128]{1,0:T(8,128)(2,1)} %constant.113.clone.fwd_y2) | copy-start | bytes 98308
  38.8 4.1 %collective-permute-start = (f32[800,128]{1,0:T(8,128)S(1)}, f32[800,128]{1,0:T(8,128)S(1)}, u32[]{:S(2)}, u32[]{:S(2)}) collective-permute-start(f32[800,128]{1,0:T(8,128)S(1)} %get-tuple-element.8), channel_id=1, source_target_pairs={{0,16},{16,0},{32,48},{48,32},{64,80},{80,64},{96,112},{112,96},{1... | collective-permute-start | bytes 1228808 | tf_op jit(solution)/shard_map/ppermute | solution.py:443
  41.9 1.0 %copy-start.3 = (f32[96,128]{1,0:T(8,128)S(1)}, f32[96,128]{1,0:T(8,128)}, u32[]{:S(2)}) copy-start(f32[96,128]{1,0:T(8,128)} %constant.114.clone.base) | copy-start | bytes 147460

commit v5 on v4

--- a/solution.py
+++ b/solution.py
@@ -508,7 +508,7 @@
         y_sin,
         strength[None],
     )
-    across, along = reduce_groups()
+    along, across = reduce_groups()
     total = jnp.sum(lax.all_to_all(spread, AXES, 0, 0, axis_index_groups=across, tiled=True), axis=0)
     spread = jnp.broadcast_to(total[None], (16, 3, LANES))
     return jnp.sum(lax.all_to_all(spread, AXES, 0, 0, axis_index_groups=along, tiled=True), axis=0)

time: 74.7 us -> 73.3 us (0.981)
  blocking collectives: 25.4 us -> 23.9 us
    all_to_all x1, blocking collectives: 12.7 us -> 11.2 us  [shards(): lax.all_to_all(spread, AXES, 0, 0, axis_index_groups=across, tiled=True)]
where the time goes in v5:
time: 73.3 us; the launch traced here: 72.9 us
  blocking collectives  23.9 us (33%)
  Pallas kernels  15.8 us (22%)
  starting transfers between devices  12.8 us (17%)
  waiting for transfers between devices  11.9 us (16%)
  other arithmetic  3.53 us (5%)
  local copies, waits for them, and re-layouts  3.37 us (5%)
  between operations  1.57 us (2%)
    all_to_all x1, blocking collectives, shards(): lax.all_to_all(spread, AXES, 0, 0, axis_index_groups=along, tiled=True)  12.7 us
    all_to_all x1, blocking collectives, shards(): lax.all_to_all(spread, AXES, 0, 0, axis_index_groups=across, tiled=True)  11.2 us
    all_to_all x1, waiting for transfers between devices, shards(): lax.all_to_all(payload, AXES, 0, 0, axis_index_groups=exchange_groups(),...  11.1 us
    all_to_all x1, starting transfers between devices, shards(): lax.all_to_all(payload, AXES, 0, 0, axis_index_groups=exchange_groups(),...  10.1 us
    pallas_call x1, Pallas kernels, shards(): pl.pallas_call(density_kernel, out_shape=(halves_shape, halves_shape), in...  6.82 us
    pallas_call x1, Pallas kernels, shards(): pl.pallas_call(force_kernel, out_shape=jax.ShapeDtypeStruct((16, 3, LANES...  5.48 us
    pallas_call x1, Pallas kernels, shards(): pl.pallas_call(send_kernel, out_shape=jax.ShapeDtypeStruct((16, ROWS, LAN...  3.47 us
    ppermute x1, starting transfers between devices, shards(): arrived = lax.ppermute(other, 'band', swap)  2.71 us
  transfers between devices with their start and end apart: 2, of which 2 were waited for; matrix products, arithmetic and copies ran while one was open for 5% of the time, Pallas kernels for 0%

profile of v5, /device:TPU:1, one launch (start us, length us, event | category | flops | bytes accessed | tf_op | source)
XLA Modules:
  0.0 72.9 jit_solution(17739250289878854785)
XLA Ops:
  0.0 3.5 %sticks.1 = f32[16,88,128]{2,1,0:T(8,128)} custom-call(s32[1,144]{1,0:T(1,128)} %bitcast.24, f32[1,4,2,13824]{3,2,1,0:T(2,128)} %coefs.1, bf16[384,256]{1,0:T(8,128)(2,1)} %constant.108.clone.z_waves), custom_call_target="tpu_custom_call" | custom-call | tf_op jit(solution)/shard_map/sticks/pallas_call | solution.py:394
  3.5 10.1 %all-to-all-start = ((f32[16,88,128]{2,1,0:T(8,128)}), f32[16,88,128]{2,1,0:T(8,128)S(1)}, u32[]{:S(2)}, u32[]{:S(2)}) async-start(f32[16,88,128]{2,1,0:T(8,128)} %sticks.1), calls=%async_computation | async-start | bytes 1441792 | tf_op jit(solution)/shard_map/all_to_all | solution.py:413
  13.8 0.6 copy-done.10
  14.4 0.6 reduce_sum.45
  15.0 0.6 dynamic_slice.8
  16.9 0.1 copy-done.7
  16.9 0.0 copy-done.9
  16.9 0.1 select_reduce_fusion
  17.1 0.7 copy-done.6
  17.7 0.1 fusion.11
  17.9 0.1 pad_maximum_fusion.6
  17.9 0.1 copy.20
  18.1 0.3 cosine_multiply_fusion.1
  18.5 0.1 pad_maximum_fusion.2.x_all
  18.6 0.8 %copy-done.5 = bf16[2,128,336]{2,1,0:T(8,128)(2,1)S(1)} copy-done((bf16[2,128,336]{2,1,0:T(8,128)(2,1)S(1)}, bf16[2,128,336]{2,1,0:T(8,128)(2,1)}, u32[]{:S(2)}) %copy-start.5) | copy-done | bytes 172056
  19.4 0.3 broadcast_multiply_fusion.1
  19.7 0.1 pad_maximum_fusion.3
  19.8 0.3 cosine_multiply_fusion.2
  20.2 0.1 reduce-precision_convert_fusion.1
  20.4 0.4 copy-done.11
  20.8 11.1 %all-to-all-done = f32[16,88,128]{2,1,0:T(8,128)S(1)} async-done(((f32[16,88,128]{2,1,0:T(8,128)}), f32[16,88,128]{2,1,0:T(8,128)S(1)}, u32[]{:S(2)}, u32[]{:S(2)}) %all-to-all-start) | async-done | bytes 720928 | tf_op jit(solution)/shard_map/all_to_all | solution.py:413
  32.0 6.8 %density.1 = (f32[800,128]{1,0:T(8,128)S(1)}, f32[800,128]{1,0:T(8,128)S(1)}) custom-call(f32[4]{0:T(128)S(1)} %multiply_bitcast_fusion.factors, f32[1408,128]{1,0:T(8,128)S(1)} %bitcast.18, bf16[2,256,256]{2,1,0:T(8,128)(2,1)S(1)} %copy-done, bf16[112,192]{1,0:T(8,128)(2,1)S(1)} %copy-done.2, bf16[256,128]{1,0:T(8,128)(2,1)S(1)} %copy-done.1, ...), custom_call_target="tpu_custom_call" | custom-call | tf_op jit(solution)/shard_map/density/pallas_call | solution.py:424
  38.8 2.7 %collective-permute-start = (f32[800,128]{1,0:T(8,128)S(1)}, f32[800,128]{1,0:T(8,128)S(1)}, u32[]{:S(2)}, u32[]{:S(2)}) collective-permute-start(f32[800,128]{1,0:T(8,128)S(1)} %get-tuple-element.8), channel_id=1, source_target_pairs={{0,16},{16,0},{32,48},{48,32},{64,80},{80,64},{96,112},{112,96},{1... | collective-permute-start | bytes 1228808 | tf_op jit(solution)/shard_map/ppermute | solution.py:443
  41.5 0.1 pad_maximum_fusion.5.wave_z
  41.6 0.1 reduce-precision_convert_fusion
  41.7 0.2 pad_maximum_fusion.1.near_z
  41.9 0.1 pad_maximum_fusion.atom_z
  42.0 0.8 %collective-permute-done.arrived = f32[800,128]{1,0:T(8,128)S(1)} collective-permute-done((f32[800,128]{1,0:T(8,128)S(1)}, f32[800,128]{1,0:T(8,128)S(1)}, u32[]{:S(2)}, u32[]{:S(2)}) %collective-permute-start) | collective-permute-done | bytes 409632 | tf_op jit(solution)/shard_map/ppermute | solution.py:443
  42.9 5.5 %force.1 = f32[16,3,128]{2,1,0:T(4,128)S(1)} custom-call(f32[32]{0:T(128)S(1)} %fusion.18.gx2, f32[800,128]{1,0:T(8,128)S(1)} %get-tuple-element.7.own, f32[800,128]{1,0:T(8,128)S(1)} %collective-permute-done.arrived, f32[96,128]{1,0:T(8,128)S(1)} %copy-done.3, bf16[192,48]{1,0:T(8,128)(2,1)S(1)} %pad_maximum_fusion.5.wave_z, ...), custom_call_target="tpu_custom_call" | custom-call | tf_op jit(solution)/shard_map/force/pallas_call | solution.py:487
  48.3 11.2 %all_to_all.15 = f32[16,3,128]{2,1,0:T(4,128)S(1)} all-to-all(f32[16,3,128]{2,1,0:T(4,128)S(1)} %force.1), channel_id=1, replica_groups={{0,16,2,18,4,20,6,22,8,24,10,26,12,28,14,30},{32,48,34,50,36,52,38,54,4..., dimensions={0} | all-to-all | bytes 49152 | tf_op jit(solution)/shard_map/all_to_all | solution.py:512
  59.6 12.7 %all_to_all.16 = f32[16,3,128]{2,1,0:T(4,128)S(1)} all-to-all(f32[16,3,128]{2,1,0:T(4,128)S(1)} %broadcast_in_dim.93), channel_id=1, replica_groups={{0,32,64,96,1,33,65,97,128,160,192,224,129,161,193,225},{16,48,80,112,1..., dimensions={0} | all-to-all | bytes 49152 | tf_op jit(solution)/shard_map/all_to_all | solution.py:514
  72.3 0.6 reduce_sum.49
  (35 shorter events, 0.2 us)
Async XLA Ops:
  3.5 28.4 %all-to-all-start = ((f32[16,88,128]{2,1,0:T(8,128)}), f32[16,88,128]{2,1,0:T(8,128)S(1)}, u32[]{:S(2)}, u32[]{:S(2)}) async-start(f32[16,88,128]{2,1,0:T(8,128)} %sticks.1), calls=%async_computation | async-start | bytes 1441792 | tf_op jit(solution)/shard_map/all_to_all | solution.py:413
  13.8 0.7 copy-start.10
  16.3 0.7 copy-start.7
  16.3 0.7 copy-start.8
  16.3 0.7 copy-start.9
  17.0 0.7 copy-start.6
  18.4 0.9 %copy-start.5 = (bf16[2,128,336]{2,1,0:T(8,128)(2,1)S(1)}, bf16[2,128,336]{2,1,0:T(8,128)(2,1)}, u32[]{:S(2)}) copy-start(bf16[2,128,336]{2,1,0:T(8,128)(2,1)} %constant.109.clone) | copy-start | bytes 516100
  20.2 0.7 copy-start.11
  20.2 11.7 %copy-start = (bf16[2,256,256]{2,1,0:T(8,128)(2,1)S(1)}, bf16[2,256,256]{2,1,0:T(8,128)(2,1)}, u32[]{:S(2)}) copy-start(bf16[2,256,256]{2,1,0:T(8,128)(2,1)} %constant.110.clone.inv_y) | copy-start | bytes 786436
  20.2 11.7 %copy-start.1 = (bf16[256,128]{1,0:T(8,128)(2,1)S(1)}, bf16[256,128]{1,0:T(8,128)(2,1)}, u32[]{:S(2)}) copy-start(bf16[256,128]{1,0:T(8,128)(2,1)} %constant.112.clone.fwd_y1) | copy-start | bytes 196612
  20.2 11.7 %copy-start.2 = (bf16[112,192]{1,0:T(8,128)(2,1)S(1)}, bf16[112,192]{1,0:T(8,128)(2,1)}, u32[]{:S(2)}) copy-start(bf16[112,192]{1,0:T(8,128)(2,1)} %constant.111.clone.inv_x) | copy-start | bytes 129028
  20.2 11.7 %copy-start.4 = (bf16[128,128]{1,0:T(8,128)(2,1)S(1)}, bf16[128,128]{1,0:T(8,128)(2,1)}, u32[]{:S(2)}) copy-start(bf16[128,128]{1,0:T(8,128)(2,1)} %constant.113.clone.fwd_y2) | copy-start | bytes 98308
  38.8 4.1 %collective-permute-start = (f32[800,128]{1,0:T(8,128)S(1)}, f32[800,128]{1,0:T(8,128)S(1)}, u32[]{:S(2)}, u32[]{:S(2)}) collective-permute-start(f32[800,128]{1,0:T(8,128)S(1)} %get-tuple-element.8), channel_id=1, source_target_pairs={{0,16},{16,0},{32,48},{48,32},{64,80},{80,64},{96,112},{112,96},{1... | collective-permute-start | bytes 1228808 | tf_op jit(solution)/shard_map/ppermute | solution.py:443
  41.9 1.0 %copy-start.3 = (f32[96,128]{1,0:T(8,128)S(1)}, f32[96,128]{1,0:T(8,128)}, u32[]{:S(2)}) copy-start(f32[96,128]{1,0:T(8,128)} %constant.114.clone.base) | copy-start | bytes 147460

commit v6 on v5

--- a/solution.py
+++ b/solution.py
@@ -47,8 +47,8 @@
 
 def reduce_groups():
     ranks = np.arange(256).reshape(2, 4, 2, 8, 2)
-    across = ranks.transpose(3, 2, 0, 4, 1).reshape(16, 16)
-    along = ranks.transpose(0, 4, 1, 3, 2).reshape(16, 16)
+    across = ranks.transpose(3, 2, 4, 0, 1).reshape(16, 16)
+    along = ranks.transpose(0, 1, 4, 2, 3).reshape(16, 16)
     return across.tolist(), along.tolist()
 
 

time: 73.3 us -> 73 us (level)
  no operation moved by 1% of the time
where the time goes in v6:
time: 73 us; the launch traced here: 72.6 us
  blocking collectives  23.6 us (32%)
  Pallas kernels  15.8 us (22%)
  starting transfers between devices  12.8 us (18%)
  waiting for transfers between devices  11.9 us (16%)
  other arithmetic  3.53 us (5%)
  local copies, waits for them, and re-layouts  3.37 us (5%)
  between operations  1.57 us (2%)
    all_to_all x1, blocking collectives, shards(): lax.all_to_all(spread, AXES, 0, 0, axis_index_groups=along, tiled=True)  12.7 us
    all_to_all x1, waiting for transfers between devices, shards(): lax.all_to_all(payload, AXES, 0, 0, axis_index_groups=exchange_groups(),...  11.1 us
    all_to_all x1, blocking collectives, shards(): lax.all_to_all(spread, AXES, 0, 0, axis_index_groups=across, tiled=True)  10.9 us
    all_to_all x1, starting transfers between devices, shards(): lax.all_to_all(payload, AXES, 0, 0, axis_index_groups=exchange_groups(),...  10.1 us
    pallas_call x1, Pallas kernels, shards(): pl.pallas_call(density_kernel, out_shape=(halves_shape, halves_shape), in...  6.82 us
    pallas_call x1, Pallas kernels, shards(): pl.pallas_call(force_kernel, out_shape=jax.ShapeDtypeStruct((16, 3, LANES...  5.48 us
    pallas_call x1, Pallas kernels, shards(): pl.pallas_call(send_kernel, out_shape=jax.ShapeDtypeStruct((16, ROWS, LAN...  3.47 us
    ppermute x1, starting transfers between devices, shards(): arrived = lax.ppermute(other, 'band', swap)  2.71 us
  transfers between devices with their start and end apart: 2, of which 2 were waited for; matrix products, arithmetic and copies ran while one was open for 5% of the time, Pallas kernels for 0%

profile of v6, /device:TPU:1, one launch (start us, length us, event | category | flops | bytes accessed | tf_op | source)
XLA Modules:
  0.0 72.6 jit_solution(3295867694954871568)
XLA Ops:
  0.0 3.5 %sticks.1 = f32[16,88,128]{2,1,0:T(8,128)} custom-call(s32[1,144]{1,0:T(1,128)} %bitcast.24, f32[1,4,2,13824]{3,2,1,0:T(2,128)} %coefs.1, bf16[384,256]{1,0:T(8,128)(2,1)} %constant.108.clone.z_waves), custom_call_target="tpu_custom_call" | custom-call | tf_op jit(solution)/shard_map/sticks/pallas_call | solution.py:394
  3.5 10.1 %all-to-all-start = ((f32[16,88,128]{2,1,0:T(8,128)}), f32[16,88,128]{2,1,0:T(8,128)S(1)}, u32[]{:S(2)}, u32[]{:S(2)}) async-start(f32[16,88,128]{2,1,0:T(8,128)} %sticks.1), calls=%async_computation | async-start | bytes 1441792 | tf_op jit(solution)/shard_map/all_to_all | solution.py:413
  13.8 0.6 copy-done.10
  14.4 0.6 reduce_sum.45
  15.0 0.6 dynamic_slice.8
  16.9 0.1 copy-done.7
  16.9 0.0 copy-done.8
  16.9 0.1 select_reduce_fusion
  17.1 0.7 copy-done.6
  17.7 0.1 fusion.11
  17.9 0.1 pad_maximum_fusion.6
  17.9 0.1 copy.20
  18.1 0.3 cosine_multiply_fusion.1
  18.5 0.1 pad_maximum_fusion.2.x_all
  18.6 0.8 %copy-done.5 = bf16[2,128,336]{2,1,0:T(8,128)(2,1)S(1)} copy-done((bf16[2,128,336]{2,1,0:T(8,128)(2,1)S(1)}, bf16[2,128,336]{2,1,0:T(8,128)(2,1)}, u32[]{:S(2)}) %copy-start.5) | copy-done | bytes 172056
  19.4 0.3 broadcast_multiply_fusion.1
  19.7 0.1 pad_maximum_fusion.3
  19.8 0.3 cosine_multiply_fusion.2
  20.2 0.1 reduce-precision_convert_fusion.1
  20.4 0.4 copy-done.11
  20.8 11.1 %all-to-all-done = f32[16,88,128]{2,1,0:T(8,128)S(1)} async-done(((f32[16,88,128]{2,1,0:T(8,128)}), f32[16,88,128]{2,1,0:T(8,128)S(1)}, u32[]{:S(2)}, u32[]{:S(2)}) %all-to-all-start) | async-done | bytes 720928 | tf_op jit(solution)/shard_map/all_to_all | solution.py:413
  32.0 6.8 %density.1 = (f32[800,128]{1,0:T(8,128)S(1)}, f32[800,128]{1,0:T(8,128)S(1)}) custom-call(f32[4]{0:T(128)S(1)} %multiply_bitcast_fusion.factors, f32[1408,128]{1,0:T(8,128)S(1)} %bitcast.18, bf16[2,256,256]{2,1,0:T(8,128)(2,1)S(1)} %copy-done, bf16[112,192]{1,0:T(8,128)(2,1)S(1)} %copy-done.2, bf16[256,128]{1,0:T(8,128)(2,1)S(1)} %copy-done.1, ...), custom_call_target="tpu_custom_call" | custom-call | tf_op jit(solution)/shard_map/density/pallas_call | solution.py:424
  38.8 2.7 %collective-permute-start = (f32[800,128]{1,0:T(8,128)S(1)}, f32[800,128]{1,0:T(8,128)S(1)}, u32[]{:S(2)}, u32[]{:S(2)}) collective-permute-start(f32[800,128]{1,0:T(8,128)S(1)} %get-tuple-element.8), channel_id=1, source_target_pairs={{0,16},{16,0},{32,48},{48,32},{64,80},{80,64},{96,112},{112,96},{1... | collective-permute-start | bytes 1228808 | tf_op jit(solution)/shard_map/ppermute | solution.py:443
  41.5 0.1 pad_maximum_fusion.5.wave_z
  41.6 0.1 reduce-precision_convert_fusion
  41.7 0.2 pad_maximum_fusion.1.near_z
  41.9 0.1 pad_maximum_fusion.atom_z
  42.0 0.8 %collective-permute-done.arrived = f32[800,128]{1,0:T(8,128)S(1)} collective-permute-done((f32[800,128]{1,0:T(8,128)S(1)}, f32[800,128]{1,0:T(8,128)S(1)}, u32[]{:S(2)}, u32[]{:S(2)}) %collective-permute-start) | collective-permute-done | bytes 409632 | tf_op jit(solution)/shard_map/ppermute | solution.py:443
  42.9 5.5 %force.1 = f32[16,3,128]{2,1,0:T(4,128)S(1)} custom-call(f32[32]{0:T(128)S(1)} %fusion.18.gx2, f32[800,128]{1,0:T(8,128)S(1)} %get-tuple-element.7.own, f32[800,128]{1,0:T(8,128)S(1)} %collective-permute-done.arrived, f32[96,128]{1,0:T(8,128)S(1)} %copy-done.3, bf16[192,48]{1,0:T(8,128)(2,1)S(1)} %pad_maximum_fusion.5.wave_z, ...), custom_call_target="tpu_custom_call" | custom-call | tf_op jit(solution)/shard_map/force/pallas_call | solution.py:487
  48.3 10.9 %all_to_all.15 = f32[16,3,128]{2,1,0:T(4,128)S(1)} all-to-all(f32[16,3,128]{2,1,0:T(4,128)S(1)} %force.1), channel_id=1, replica_groups={{0,2,4,6,8,10,12,14,16,18,20,22,24,26,28,30},{1,3,5,7,9,11,13,15,17,19,..., dimensions={0} | all-to-all | bytes 49152 | tf_op jit(solution)/shard_map/all_to_all | solution.py:512
  59.3 12.7 %all_to_all.16 = f32[16,3,128]{2,1,0:T(4,128)S(1)} all-to-all(f32[16,3,128]{2,1,0:T(4,128)S(1)} %broadcast_in_dim.93), channel_id=1, replica_groups={{0,32,64,96,128,160,192,224,1,33,65,97,129,161,193,225},{16,48,80,112,1..., dimensions={0} | all-to-all | bytes 49152 | tf_op jit(solution)/shard_map/all_to_all | solution.py:514
  72.0 0.6 reduce_sum.49
  (35 shorter events, 0.2 us)
Async XLA Ops:
  3.5 28.4 %all-to-all-start = ((f32[16,88,128]{2,1,0:T(8,128)}), f32[16,88,128]{2,1,0:T(8,128)S(1)}, u32[]{:S(2)}, u32[]{:S(2)}) async-start(f32[16,88,128]{2,1,0:T(8,128)} %sticks.1), calls=%async_computation | async-start | bytes 1441792 | tf_op jit(solution)/shard_map/all_to_all | solution.py:413
  13.8 0.7 copy-start.10
  16.3 0.7 copy-start.7
  16.3 0.7 copy-start.8
  16.3 0.7 copy-start.9
  17.0 0.7 copy-start.6
  18.4 0.9 %copy-start.5 = (bf16[2,128,336]{2,1,0:T(8,128)(2,1)S(1)}, bf16[2,128,336]{2,1,0:T(8,128)(2,1)}, u32[]{:S(2)}) copy-start(bf16[2,128,336]{2,1,0:T(8,128)(2,1)} %constant.109.clone) | copy-start | bytes 516100
  20.2 0.7 copy-start.11
  20.2 11.7 %copy-start = (bf16[2,256,256]{2,1,0:T(8,128)(2,1)S(1)}, bf16[2,256,256]{2,1,0:T(8,128)(2,1)}, u32[]{:S(2)}) copy-start(bf16[2,256,256]{2,1,0:T(8,128)(2,1)} %constant.110.clone.inv_y) | copy-start | bytes 786436
  20.2 11.7 %copy-start.1 = (bf16[256,128]{1,0:T(8,128)(2,1)S(1)}, bf16[256,128]{1,0:T(8,128)(2,1)}, u32[]{:S(2)}) copy-start(bf16[256,128]{1,0:T(8,128)(2,1)} %constant.112.clone.fwd_y1) | copy-start | bytes 196612
  20.2 11.7 %copy-start.2 = (bf16[112,192]{1,0:T(8,128)(2,1)S(1)}, bf16[112,192]{1,0:T(8,128)(2,1)}, u32[]{:S(2)}) copy-start(bf16[112,192]{1,0:T(8,128)(2,1)} %constant.111.clone.inv_x) | copy-start | bytes 129028
  20.2 11.7 %copy-start.4 = (bf16[128,128]{1,0:T(8,128)(2,1)S(1)}, bf16[128,128]{1,0:T(8,128)(2,1)}, u32[]{:S(2)}) copy-start(bf16[128,128]{1,0:T(8,128)(2,1)} %constant.113.clone.fwd_y2) | copy-start | bytes 98308
  38.8 4.1 %collective-permute-start = (f32[800,128]{1,0:T(8,128)S(1)}, f32[800,128]{1,0:T(8,128)S(1)}, u32[]{:S(2)}, u32[]{:S(2)}) collective-permute-start(f32[800,128]{1,0:T(8,128)S(1)} %get-tuple-element.8), channel_id=1, source_target_pairs={{0,16},{16,0},{32,48},{48,32},{64,80},{80,64},{96,112},{112,96},{1... | collective-permute-start | bytes 1228808 | tf_op jit(solution)/shard_map/ppermute | solution.py:443
  41.9 1.0 %copy-start.3 = (f32[96,128]{1,0:T(8,128)S(1)}, f32[96,128]{1,0:T(8,128)}, u32[]{:S(2)}) copy-start(f32[96,128]{1,0:T(8,128)} %constant.114.clone.base) | copy-start | bytes 147460

commit v7 on v6

--- a/solution.py
+++ b/solution.py
@@ -23,6 +23,7 @@
 SPARE = 15
 ROWS = 88
 NEAR = 80
+LAST = 32
 HELD = 72
 FOLD = 56
 GROUPS = 36
@@ -350,7 +351,7 @@
 
 
 def force_kernel(
-    gx2, own, arrived, base, wave_z, atom_z, near_z, x_all, y_cos, y_sin, strength, out, acc, turn
+    gx2, own, arrived, base, wave_z, atom_z, near_z, last_z, x_all, y_cos, y_sin, strength, out, acc, turn
 ):
     acc[...] = jnp.zeros_like(acc)
     turn[...] = x_all[...]
@@ -380,7 +381,8 @@
         return 0
 
     lax.fori_loop(0, 14, lambda slot, _: step(slot, ZSPAN, atom_z), 0, unroll=14)
-    lax.fori_loop(14, SLOTS, lambda slot, _: step(slot, NEAR, near_z), 0, unroll=11)
+    lax.fori_loop(14, 23, lambda slot, _: step(slot, NEAR, near_z), 0, unroll=9)
+    lax.fori_loop(23, SLOTS, lambda slot, _: step(slot, LAST, last_z), 0, unroll=2)
     parts = [acc[0] * y_cos[...], acc[1] * y_sin[...], acc[2] * y_cos[...]]
     rows = [-strength[...] * jnp.sum(part.T, axis=0, keepdims=True) for part in parts]
     block = jnp.concatenate(rows, 0)
@@ -487,7 +489,7 @@
     spread = pl.pallas_call(
         force_kernel,
         out_shape=jax.ShapeDtypeStruct((16, 3, LANES), jnp.float32),
-        in_specs=[SMEM] + [VMEM] * 10,
+        in_specs=[SMEM] + [VMEM] * 11,
         out_specs=VMEM,
         scratch_shapes=[
             pltpu.VMEM((3, 128, 128), jnp.float32),
@@ -503,6 +505,7 @@
         wave_z,
         atom_table(ZSPAN),
         atom_table(NEAR),
+        atom_table(LAST),
         x_all,
         y_cos,
         y_sin,

time: 73 us -> 73.1 us (level)
  waiting for transfers between devices: 11.9 us -> 11.1 us
    all_to_all x1, waiting for transfers between devices: 11.1 us -> 10.3 us  [shards(): lax.all_to_all(payload, AXES, 0, 0, axis_index_groups=exchange_groups(),...]
where the time goes in v7:
time: 73.1 us; the launch traced here: 72.7 us
  blocking collectives  23.6 us (32%)
  Pallas kernels  15.9 us (22%)
  starting transfers between devices  12.8 us (18%)
  waiting for transfers between devices  11.1 us (15%)
  local copies, waits for them, and re-layouts  3.96 us (5%)
  other arithmetic  3.77 us (5%)
  between operations  1.57 us (2%)
    all_to_all x1, blocking collectives, shards(): lax.all_to_all(spread, AXES, 0, 0, axis_index_groups=along, tiled=True)  12.7 us
    all_to_all x1, blocking collectives, shards(): lax.all_to_all(spread, AXES, 0, 0, axis_index_groups=across, tiled=True)  10.9 us
    all_to_all x1, waiting for transfers between devices, shards(): lax.all_to_all(payload, AXES, 0, 0, axis_index_groups=exchange_groups(),...  10.3 us
    all_to_all x1, starting transfers between devices, shards(): lax.all_to_all(payload, AXES, 0, 0, axis_index_groups=exchange_groups(),...  10.1 us
    pallas_call x1, Pallas kernels, shards(): pl.pallas_call(density_kernel, out_shape=(halves_shape, halves_shape), in...  6.81 us
    pallas_call x1, Pallas kernels, shards(): pl.pallas_call(force_kernel, out_shape=jax.ShapeDtypeStruct((16, 3, LANES...  5.6 us
    pallas_call x1, Pallas kernels, shards(): pl.pallas_call(send_kernel, out_shape=jax.ShapeDtypeStruct((16, ROWS, LAN...  3.47 us
    unnamed x24, local copies, waits for them, and re-layouts  3.24 us
  transfers between devices with their start and end apart: 2, of which 2 were waited for; matrix products, arithmetic and copies ran while one was open for 5% of the time, Pallas kernels for 0%

profile of v7, /device:TPU:1, one launch (start us, length us, event | category | flops | bytes accessed | tf_op | source)
XLA Modules:
  0.0 72.7 jit_solution(3990215445151157819)
XLA Ops:
  0.0 3.5 %sticks.1 = f32[16,88,128]{2,1,0:T(8,128)} custom-call(s32[1,144]{1,0:T(1,128)} %bitcast.32, f32[1,4,2,13824]{3,2,1,0:T(2,128)} %coefs.1, bf16[384,256]{1,0:T(8,128)(2,1)} %constant.108.clone.z_waves), custom_call_target="tpu_custom_call" | custom-call | tf_op jit(solution)/shard_map/sticks/pallas_call | solution.py:396
  3.5 10.1 %all-to-all-start = ((f32[16,88,128]{2,1,0:T(8,128)}), f32[16,88,128]{2,1,0:T(8,128)S(1)}, u32[]{:S(2)}, u32[]{:S(2)}) async-start(f32[16,88,128]{2,1,0:T(8,128)} %sticks.1), calls=%async_computation | async-start | bytes 1441792 | tf_op jit(solution)/shard_map/all_to_all | solution.py:415
  13.8 0.6 copy-done.10
  14.4 0.6 reduce_sum.45
  15.0 0.6 dynamic_slice.8
  16.9 0.1 fusion.12
  17.1 0.1 copy.20
  17.2 0.6 copy-done.6
  17.9 0.6 copy-done.7
  18.6 0.1 select_reduce_fusion
  18.7 0.3 cosine_multiply_fusion.1
  19.1 0.1 pad_maximum_fusion.3.x_all
  19.2 0.8 %copy-done.5 = bf16[2,128,336]{2,1,0:T(8,128)(2,1)S(1)} copy-done((bf16[2,128,336]{2,1,0:T(8,128)(2,1)S(1)}, bf16[2,128,336]{2,1,0:T(8,128)(2,1)}, u32[]{:S(2)}) %copy-start.5) | copy-done | bytes 172056
  20.0 0.3 cosine_multiply_fusion.2
  20.3 0.1 reduce-precision_convert_fusion.2
  20.4 0.1 pad_maximum_fusion.2.last_z
  20.6 0.3 broadcast_multiply_fusion.1
  20.9 0.1 pad_maximum_fusion.4
  21.1 0.1 reduce-precision_convert_fusion.1
  21.2 0.4 copy-done.11
  21.7 10.3 %all-to-all-done = f32[16,88,128]{2,1,0:T(8,128)S(1)} async-done(((f32[16,88,128]{2,1,0:T(8,128)}), f32[16,88,128]{2,1,0:T(8,128)S(1)}, u32[]{:S(2)}, u32[]{:S(2)}) %all-to-all-start) | async-done | bytes 720928 | tf_op jit(solution)/shard_map/all_to_all | solution.py:415
  31.9 6.8 %density.1 = (f32[800,128]{1,0:T(8,128)S(1)}, f32[800,128]{1,0:T(8,128)S(1)}) custom-call(f32[4]{0:T(128)S(1)} %multiply_bitcast_fusion.factors, f32[1408,128]{1,0:T(8,128)S(1)} %bitcast.22, bf16[2,256,256]{2,1,0:T(8,128)(2,1)S(1)} %copy-done, bf16[112,192]{1,0:T(8,128)(2,1)S(1)} %copy-done.2, bf16[256,128]{1,0:T(8,128)(2,1)S(1)} %copy-done.1, ...), custom_call_target="tpu_custom_call" | custom-call | tf_op jit(solution)/shard_map/density/pallas_call | solution.py:426
  38.8 2.7 %collective-permute-start = (f32[800,128]{1,0:T(8,128)S(1)}, f32[800,128]{1,0:T(8,128)S(1)}, u32[]{:S(2)}, u32[]{:S(2)}) collective-permute-start(f32[800,128]{1,0:T(8,128)S(1)} %get-tuple-element.8), channel_id=1, source_target_pairs={{0,16},{16,0},{32,48},{48,32},{64,80},{80,64},{96,112},{112,96},{1... | collective-permute-start | bytes 1228808 | tf_op jit(solution)/shard_map/ppermute | solution.py:445
  41.5 0.1 pad_maximum_fusion.6.wave_z
  41.6 0.1 reduce-precision_convert_fusion
  41.7 0.2 pad_maximum_fusion.1.near_z
  41.9 0.1 pad_maximum_fusion.atom_z
  42.0 0.8 %collective-permute-done.arrived = f32[800,128]{1,0:T(8,128)S(1)} collective-permute-done((f32[800,128]{1,0:T(8,128)S(1)}, f32[800,128]{1,0:T(8,128)S(1)}, u32[]{:S(2)}, u32[]{:S(2)}) %collective-permute-start) | collective-permute-done | bytes 409632 | tf_op jit(solution)/shard_map/ppermute | solution.py:445
  42.8 5.6 %force.1 = f32[16,3,128]{2,1,0:T(4,128)S(1)} custom-call(f32[32]{0:T(128)S(1)} %fusion.19.gx2, f32[800,128]{1,0:T(8,128)S(1)} %get-tuple-element.7.own, f32[800,128]{1,0:T(8,128)S(1)} %collective-permute-done.arrived, f32[96,128]{1,0:T(8,128)S(1)} %copy-done.3, bf16[192,48]{1,0:T(8,128)(2,1)S(1)} %pad_maximum_fusion.6.wave_z, ...), custom_call_target="tpu_custom_call" | custom-call | tf_op jit(solution)/shard_map/force/pallas_call | solution.py:489
  48.5 10.9 %all_to_all.15 = f32[16,3,128]{2,1,0:T(4,128)S(1)} all-to-all(f32[16,3,128]{2,1,0:T(4,128)S(1)} %force.1), channel_id=1, replica_groups={{0,2,4,6,8,10,12,14,16,18,20,22,24,26,28,30},{1,3,5,7,9,11,13,15,17,19,..., dimensions={0} | all-to-all | bytes 49152 | tf_op jit(solution)/shard_map/all_to_all | solution.py:515
  59.4 12.7 %all_to_all.16 = f32[16,3,128]{2,1,0:T(4,128)S(1)} all-to-all(f32[16,3,128]{2,1,0:T(4,128)S(1)} %broadcast_in_dim.93), channel_id=1, replica_groups={{0,32,64,96,128,160,192,224,1,33,65,97,129,161,193,225},{16,48,80,112,1..., dimensions={0} | all-to-all | bytes 49152 | tf_op jit(solution)/shard_map/all_to_all | solution.py:517
  72.1 0.6 reduce_sum.49
  (37 shorter events, 0.3 us)
Async XLA Ops:
  3.5 28.4 %all-to-all-start = ((f32[16,88,128]{2,1,0:T(8,128)}), f32[16,88,128]{2,1,0:T(8,128)S(1)}, u32[]{:S(2)}, u32[]{:S(2)}) async-start(f32[16,88,128]{2,1,0:T(8,128)} %sticks.1), calls=%async_computation | async-start | bytes 1441792 | tf_op jit(solution)/shard_map/all_to_all | solution.py:415
  13.7 0.7 copy-start.10
  17.2 0.7 copy-start.6
  17.9 0.7 copy-start.7
  17.9 0.7 copy-start.8
  17.9 0.7 copy-start.9
  19.0 0.9 %copy-start.5 = (bf16[2,128,336]{2,1,0:T(8,128)(2,1)S(1)}, bf16[2,128,336]{2,1,0:T(8,128)(2,1)}, u32[]{:S(2)}) copy-start(bf16[2,128,336]{2,1,0:T(8,128)(2,1)} %constant.109.clone) | copy-start | bytes 516100
  21.0 0.7 copy-start.11
  21.0 10.9 %copy-start = (bf16[2,256,256]{2,1,0:T(8,128)(2,1)S(1)}, bf16[2,256,256]{2,1,0:T(8,128)(2,1)}, u32[]{:S(2)}) copy-start(bf16[2,256,256]{2,1,0:T(8,128)(2,1)} %constant.110.clone.inv_y) | copy-start | bytes 786436
  21.0 10.9 %copy-start.1 = (bf16[256,128]{1,0:T(8,128)(2,1)S(1)}, bf16[256,128]{1,0:T(8,128)(2,1)}, u32[]{:S(2)}) copy-start(bf16[256,128]{1,0:T(8,128)(2,1)} %constant.112.clone.fwd_y1) | copy-start | bytes 196612
  21.0 10.9 %copy-start.2 = (bf16[112,192]{1,0:T(8,128)(2,1)S(1)}, bf16[112,192]{1,0:T(8,128)(2,1)}, u32[]{:S(2)}) copy-start(bf16[112,192]{1,0:T(8,128)(2,1)} %constant.111.clone.inv_x) | copy-start | bytes 129028
  21.1 10.9 %copy-start.4 = (bf16[128,128]{1,0:T(8,128)(2,1)S(1)}, bf16[128,128]{1,0:T(8,128)(2,1)}, u32[]{:S(2)}) copy-start(bf16[128,128]{1,0:T(8,128)(2,1)} %constant.113.clone.fwd_y2) | copy-start | bytes 98308
  38.8 4.1 %collective-permute-start = (f32[800,128]{1,0:T(8,128)S(1)}, f32[800,128]{1,0:T(8,128)S(1)}, u32[]{:S(2)}, u32[]{:S(2)}) collective-permute-start(f32[800,128]{1,0:T(8,128)S(1)} %get-tuple-element.8), channel_id=1, source_target_pairs={{0,16},{16,0},{32,48},{48,32},{64,80},{80,64},{96,112},{112,96},{1... | collective-permute-start | bytes 1228808 | tf_op jit(solution)/shard_map/ppermute | solution.py:445
  41.9 1.0 %copy-start.3 = (f32[96,128]{1,0:T(8,128)S(1)}, f32[96,128]{1,0:T(8,128)}, u32[]{:S(2)}) copy-start(f32[96,128]{1,0:T(8,128)} %constant.114.clone.base) | copy-start | bytes 147460

commit v8 on v6

--- a/solution.py
+++ b/solution.py
@@ -18,7 +18,7 @@
 LANES = 128
 PLANES = 12
 SLOTS = 25
-SIDE_ROWS = SLOTS * 16
+SIDE_ROWS = SLOTS * 12
 STICK_LIMIT = 113
 SPARE = 15
 ROWS = 88
@@ -300,11 +300,6 @@
         return 0
 
     lax.fori_loop(0, 25, place, 0, unroll=25)
-    clear = jnp.zeros((2 * SLOTS, 128), jnp.float32)
-    for row in range(PLANES, 16):
-        own[pl.ds(row, 2 * SLOTS, stride=16), :] = clear
-        other[pl.ds(row, 2 * SLOTS, stride=16), :] = clear
-
     def waves(plane, _):
         even = jnp.zeros((FOLD, 128), jnp.float32)
         odd = jnp.zeros((FOLD, 128), jnp.float32)
@@ -338,8 +333,8 @@
             for member in range(2):
                 plane = group * 4 + pair * 2 + member
                 lanes = slice(member * 128, member * 128 + 128)
-                cosine = pl.ds(plane, SLOTS, stride=16)
-                sine = pl.ds(plane + SIDE_ROWS, SLOTS, stride=16)
+                cosine = pl.ds(plane, SLOTS, stride=12)
+                sine = pl.ds(plane + SIDE_ROWS, SLOTS, stride=12)
                 own[cosine, :] = out[0:SLOTS, lanes]
                 own[sine, :] = out[32 : 32 + SLOTS, lanes]
                 other[cosine, :] = out[64 : 64 + SLOTS, lanes]
@@ -356,10 +351,11 @@
     turn[...] = x_all[...]
 
     def step(slot, reach, phases):
-        start = pl.multiple_of(slot * 16, 16)
-        first, second = pl.ds(start, 16), pl.ds(start + SIDE_ROWS, 16)
+        first = slice(slot * PLANES, slot * PLANES + PLANES)
+        second = slice(SIDE_ROWS + slot * PLANES, SIDE_ROWS + slot * PLANES + PLANES)
         pair = [own[first, :] + arrived[first, :], own[second, :] + arrived[second, :]]
-        high, low = halves(jnp.concatenate(pair, 1))
+        pair = jnp.concatenate([jnp.concatenate(pair, 1), jnp.zeros((4, 256), jnp.float32)], 0)
+        high, low = halves(pair)
         waves = wave_z[...]
         if reach < ZSPAN:
             waves = jnp.concatenate([waves[:reach], waves[ZSPAN : ZSPAN + reach]], 0)
@@ -379,8 +375,8 @@
         turn[...] = pltpu.roll(table, 127, 1)
         return 0
 
-    lax.fori_loop(0, 14, lambda slot, _: step(slot, ZSPAN, atom_z), 0, unroll=14)
-    lax.fori_loop(14, SLOTS, lambda slot, _: step(slot, NEAR, near_z), 0, unroll=11)
+    for slot in range(SLOTS):
+        step(slot, *((ZSPAN, atom_z) if slot < 14 else (NEAR, near_z)))
     parts = [acc[0] * y_cos[...], acc[1] * y_sin[...], acc[2] * y_cos[...]]
     rows = [-strength[...] * jnp.sum(part.T, axis=0, keepdims=True) for part in parts]
     block = jnp.concatenate(rows, 0)

time: 73 us -> 72.7 us (level)
  no operation moved by 1% of the time
where the time goes in v8:
time: 72.7 us; the launch traced here: 72.4 us
  blocking collectives  23.6 us (32%)
  Pallas kernels  15.7 us (22%)
  starting transfers between devices  12.9 us (18%)
  waiting for transfers between devices  11.8 us (16%)
  other arithmetic  3.53 us (5%)
  local copies, waits for them, and re-layouts  3.36 us (5%)
  between operations  1.57 us (2%)
    all_to_all x1, blocking collectives, shards(): lax.all_to_all(spread, AXES, 0, 0, axis_index_groups=along, tiled=True)  12.7 us
    all_to_all x1, waiting for transfers between devices, shards(): lax.all_to_all(payload, AXES, 0, 0, axis_index_groups=exchange_groups(),...  11 us
    all_to_all x1, blocking collectives, shards(): lax.all_to_all(spread, AXES, 0, 0, axis_index_groups=across, tiled=True)  10.9 us
    all_to_all x1, starting transfers between devices, shards(): lax.all_to_all(payload, AXES, 0, 0, axis_index_groups=exchange_groups(),...  10.1 us
    pallas_call x1, Pallas kernels, shards(): pl.pallas_call(density_kernel, out_shape=(halves_shape, halves_shape), in...  6.7 us
    pallas_call x1, Pallas kernels, shards(): pl.pallas_call(force_kernel, out_shape=jax.ShapeDtypeStruct((16, 3, LANES...  5.48 us
    pallas_call x1, Pallas kernels, shards(): pl.pallas_call(send_kernel, out_shape=jax.ShapeDtypeStruct((16, ROWS, LAN...  3.47 us
    ppermute x1, starting transfers between devices, shards(): arrived = lax.ppermute(other, 'band', swap)  2.71 us
  transfers between devices with their start and end apart: 2, of which 2 were waited for; matrix products, arithmetic and copies ran while one was open for 5% of the time, Pallas kernels for 0%

profile of v8, /device:TPU:1, one launch (start us, length us, event | category | flops | bytes accessed | tf_op | source)
XLA Modules:
  0.0 72.4 jit_solution(13831047330595042723)
XLA Ops:
  0.0 3.5 %sticks.1 = f32[16,88,128]{2,1,0:T(8,128)} custom-call(s32[1,144]{1,0:T(1,128)} %bitcast.24, f32[1,4,2,13824]{3,2,1,0:T(2,128)} %coefs.1, bf16[384,256]{1,0:T(8,128)(2,1)} %constant.108.clone.z_waves), custom_call_target="tpu_custom_call" | custom-call | tf_op jit(solution)/shard_map/sticks/pallas_call | solution.py:390
  3.5 10.1 %all-to-all-start = ((f32[16,88,128]{2,1,0:T(8,128)}), f32[16,88,128]{2,1,0:T(8,128)S(1)}, u32[]{:S(2)}, u32[]{:S(2)}) async-start(f32[16,88,128]{2,1,0:T(8,128)} %sticks.1), calls=%async_computation | async-start | bytes 1441792 | tf_op jit(solution)/shard_map/all_to_all | solution.py:409
  13.8 0.6 copy-done.10
  14.4 0.6 reduce_sum.45
  15.0 0.6 dynamic_slice.8
  16.9 0.1 copy-done.7
  16.9 0.0 copy-done.8
  16.9 0.1 select_reduce_fusion
  17.1 0.7 copy-done.6
  17.7 0.1 fusion.11
  17.9 0.1 pad_maximum_fusion.6
  17.9 0.1 copy.20
  18.1 0.3 cosine_multiply_fusion.1
  18.4 0.1 pad_maximum_fusion.2.x_all
  18.6 0.8 %copy-done.5 = bf16[2,128,336]{2,1,0:T(8,128)(2,1)S(1)} copy-done((bf16[2,128,336]{2,1,0:T(8,128)(2,1)S(1)}, bf16[2,128,336]{2,1,0:T(8,128)(2,1)}, u32[]{:S(2)}) %copy-start.5) | copy-done | bytes 172056
  19.4 0.3 broadcast_multiply_fusion.1
  19.7 0.1 pad_maximum_fusion.3
  19.8 0.3 cosine_multiply_fusion.2
  20.2 0.1 reduce-precision_convert_fusion.1
  20.4 0.1 reduce-precision_convert_fusion
  20.5 0.4 copy-done.11
  21.0 11.0 %all-to-all-done = f32[16,88,128]{2,1,0:T(8,128)S(1)} async-done(((f32[16,88,128]{2,1,0:T(8,128)}), f32[16,88,128]{2,1,0:T(8,128)S(1)}, u32[]{:S(2)}, u32[]{:S(2)}) %all-to-all-start) | async-done | bytes 720928 | tf_op jit(solution)/shard_map/all_to_all | solution.py:409
  32.0 6.7 %density.1 = (f32[600,128]{1,0:T(8,128)S(1)}, f32[600,128]{1,0:T(8,128)S(1)}) custom-call(f32[4]{0:T(128)S(1)} %multiply_bitcast_fusion.factors, f32[1408,128]{1,0:T(8,128)S(1)} %bitcast.18, bf16[2,256,256]{2,1,0:T(8,128)(2,1)S(1)} %copy-done, bf16[112,192]{1,0:T(8,128)(2,1)S(1)} %copy-done.2, bf16[256,128]{1,0:T(8,128)(2,1)S(1)} %copy-done.1, ...), custom_call_target="tpu_custom_call" | custom-call | tf_op jit(solution)/shard_map/density/pallas_call | solution.py:420
  38.7 2.7 %collective-permute-start = (f32[600,128]{1,0:T(8,128)S(1)}, f32[600,128]{1,0:T(8,128)S(1)}, u32[]{:S(2)}, u32[]{:S(2)}) collective-permute-start(f32[600,128]{1,0:T(8,128)S(1)} %get-tuple-element.8), channel_id=1, source_target_pairs={{0,16},{16,0},{32,48},{48,32},{64,80},{80,64},{96,112},{112,96},{1... | collective-permute-start | bytes 921608 | tf_op jit(solution)/shard_map/ppermute | solution.py:439
  41.4 0.1 pad_maximum_fusion.5.wave_z
  41.5 0.2 pad_maximum_fusion.1.near_z
  41.7 0.1 pad_maximum_fusion.atom_z
  41.8 0.8 %collective-permute-done.arrived = f32[600,128]{1,0:T(8,128)S(1)} collective-permute-done((f32[600,128]{1,0:T(8,128)S(1)}, f32[600,128]{1,0:T(8,128)S(1)}, u32[]{:S(2)}, u32[]{:S(2)}) %collective-permute-start) | collective-permute-done | bytes 307232 | tf_op jit(solution)/shard_map/ppermute | solution.py:439
  42.6 5.5 %force.1 = f32[16,3,128]{2,1,0:T(4,128)S(1)} custom-call(f32[32]{0:T(128)S(1)} %fusion.18.gx2, f32[600,128]{1,0:T(8,128)S(1)} %get-tuple-element.7.own, f32[600,128]{1,0:T(8,128)S(1)} %collective-permute-done.arrived, f32[96,128]{1,0:T(8,128)S(1)} %copy-done.3, bf16[192,48]{1,0:T(8,128)(2,1)S(1)} %pad_maximum_fusion.5.wave_z, ...), custom_call_target="tpu_custom_call" | custom-call | tf_op jit(solution)/shard_map/force/pallas_call | solution.py:483
  48.1 10.9 %all_to_all.15 = f32[16,3,128]{2,1,0:T(4,128)S(1)} all-to-all(f32[16,3,128]{2,1,0:T(4,128)S(1)} %force.1), channel_id=1, replica_groups={{0,2,4,6,8,10,12,14,16,18,20,22,24,26,28,30},{1,3,5,7,9,11,13,15,17,19,..., dimensions={0} | all-to-all | bytes 49152 | tf_op jit(solution)/shard_map/all_to_all | solution.py:508
  59.0 12.7 %all_to_all.16 = f32[16,3,128]{2,1,0:T(4,128)S(1)} all-to-all(f32[16,3,128]{2,1,0:T(4,128)S(1)} %broadcast_in_dim.93), channel_id=1, replica_groups={{0,32,64,96,128,160,192,224,1,33,65,97,129,161,193,225},{16,48,80,112,1..., dimensions={0} | all-to-all | bytes 49152 | tf_op jit(solution)/shard_map/all_to_all | solution.py:510
  71.8 0.6 reduce_sum.49
  (35 shorter events, 0.2 us)
Async XLA Ops:
  3.5 28.4 %all-to-all-start = ((f32[16,88,128]{2,1,0:T(8,128)}), f32[16,88,128]{2,1,0:T(8,128)S(1)}, u32[]{:S(2)}, u32[]{:S(2)}) async-start(f32[16,88,128]{2,1,0:T(8,128)} %sticks.1), calls=%async_computation | async-start | bytes 1441792 | tf_op jit(solution)/shard_map/all_to_all | solution.py:409
  13.8 0.7 copy-start.10
  16.3 0.7 copy-start.7
  16.3 0.7 copy-start.8
  16.3 0.7 copy-start.9
  17.0 0.7 copy-start.6
  18.4 0.9 %copy-start.5 = (bf16[2,128,336]{2,1,0:T(8,128)(2,1)S(1)}, bf16[2,128,336]{2,1,0:T(8,128)(2,1)}, u32[]{:S(2)}) copy-start(bf16[2,128,336]{2,1,0:T(8,128)(2,1)} %constant.109.clone) | copy-start | bytes 516100
  20.3 0.7 copy-start.11
  20.3 11.6 %copy-start = (bf16[2,256,256]{2,1,0:T(8,128)(2,1)S(1)}, bf16[2,256,256]{2,1,0:T(8,128)(2,1)}, u32[]{:S(2)}) copy-start(bf16[2,256,256]{2,1,0:T(8,128)(2,1)} %constant.110.clone.inv_y) | copy-start | bytes 786436
  20.3 11.6 %copy-start.1 = (bf16[256,128]{1,0:T(8,128)(2,1)S(1)}, bf16[256,128]{1,0:T(8,128)(2,1)}, u32[]{:S(2)}) copy-start(bf16[256,128]{1,0:T(8,128)(2,1)} %constant.112.clone.fwd_y1) | copy-start | bytes 196612
  20.3 11.6 %copy-start.2 = (bf16[112,192]{1,0:T(8,128)(2,1)S(1)}, bf16[112,192]{1,0:T(8,128)(2,1)}, u32[]{:S(2)}) copy-start(bf16[112,192]{1,0:T(8,128)(2,1)} %constant.111.clone.inv_x) | copy-start | bytes 129028
  20.4 11.6 %copy-start.4 = (bf16[128,128]{1,0:T(8,128)(2,1)S(1)}, bf16[128,128]{1,0:T(8,128)(2,1)}, u32[]{:S(2)}) copy-start(bf16[128,128]{1,0:T(8,128)(2,1)} %constant.113.clone.fwd_y2) | copy-start | bytes 98308
  38.7 3.9 %collective-permute-start = (f32[600,128]{1,0:T(8,128)S(1)}, f32[600,128]{1,0:T(8,128)S(1)}, u32[]{:S(2)}, u32[]{:S(2)}) collective-permute-start(f32[600,128]{1,0:T(8,128)S(1)} %get-tuple-element.8), channel_id=1, source_target_pairs={{0,16},{16,0},{32,48},{48,32},{64,80},{80,64},{96,112},{112,96},{1... | collective-permute-start | bytes 921608 | tf_op jit(solution)/shard_map/ppermute | solution.py:439
  41.6 1.0 %copy-start.3 = (f32[96,128]{1,0:T(8,128)S(1)}, f32[96,128]{1,0:T(8,128)}, u32[]{:S(2)}) copy-start(f32[96,128]{1,0:T(8,128)} %constant.114.clone.base) | copy-start | bytes 147460
